TPU v7x, 128 devices: a whole 4x4x4 slice. The times are simulated.
128 devices in a mesh: obj: 16 (over y, z), pos: 8 (over x, core).
Axes of the slice: x: 4, y: 4, z: 4, core: 2. Of those that a mesh axis runs over, the one named last changes fastest.
Arguments:
- object_field: float32 [2, 2, 2048, 2048], P(None, None, 'obj'), may hold values from -4.2 to 4.2
- probe_modes: float32 [2, 2, 128, 128], replicated, may hold values from -6 to 6
- propagator_phase: float32 [128, 128], replicated, may hold values from -3.140625 to 3.140625
- offsets: int32 [2048, 2], P(('obj', 'pos')), may hold values from 0 to 1920, as said below
- measured: float32 [2048, 128, 128], P(('obj', 'pos')), may hold values from 0.5 to 20
Outputs:
- object_grad: float32 [2, 2, 2048, 2048], P(None, None, 'obj', 'pos')
Inputs may be any that keep to these rules, and one draw needn't show every extreme that they name: `offsets`: in each aligned block of 16 rows (the positions of one device) at most 2 rows have the same top strip, their row offset divided by 128 and rounded down, and in every block some strip is the top strip of exactly 2 rows. Every window lies inside the object: row offset at most 1920, column offset at most 1920.
All inputs are finite; a program needn't handle non-finite values.
Results may differ from a plain program's by a relative error of at most 0.0042.
Values may be sent and summed in bfloat16 or wider, within the bound.
A program may use at most 128 MiB of HBM per device.

v0:
```python
import math

import jax
import jax.numpy as jnp
from jax import lax
from jax.sharding import PartitionSpec as P

CAP = 2


def dft_blocks(length, sign):
    index_row = jnp.arange(length, dtype=jnp.int32)
    phase_index = index_row[:, None] * index_row[None, :] % length
    angles = phase_index.astype(jnp.float32) * (2.0 * math.pi / length)
    scale_by = 1.0 / math.sqrt(length)
    cosine = jnp.cos(angles) * scale_by
    sine_part = -sign * jnp.sin(angles) * scale_by
    return jnp.stack([jnp.stack([cosine, -sine_part]), jnp.stack([sine_part, cosine])])


def transform(field, blocks):
    rows_done = jnp.einsum("caij,najk->ncik", blocks, field, precision=lax.Precision.HIGHEST)
    return jnp.einsum("naik,cakl->ncil", rows_done, blocks, precision=lax.Precision.HIGHEST)


def complex_product(left_factor, right_factor):
    real_part = (
        left_factor[..., 0, :, :] * right_factor[..., 0, :, :]
        - left_factor[..., 1, :, :] * right_factor[..., 1, :, :]
    )
    imag_part = (
        left_factor[..., 0, :, :] * right_factor[..., 1, :, :]
        + left_factor[..., 1, :, :] * right_factor[..., 0, :, :]
    )
    return jnp.stack([real_part, imag_part], axis=-3)


def window_loss(windows, probe_modes, kernel, amplitude, forward, inverse):
    position_count = windows.shape[0]
    mode_count = probe_modes.shape[0]
    length = probe_modes.shape[-1]
    wavefield = jnp.broadcast_to(probe_modes[None], (position_count,) + probe_modes.shape)
    for slice_index in range(windows.shape[2]):
        wavefield = complex_product(wavefield, windows[:, None, :, slice_index])
        if slice_index + 1 < windows.shape[2]:
            spectrum = transform(
                wavefield.reshape(position_count * mode_count, 2, length, length), forward
            )
            wavefield = transform(complex_product(spectrum, kernel), inverse).reshape(
                position_count, mode_count, 2, length, length
            )
    far_field = transform(
        wavefield.reshape(position_count * mode_count, 2, length, length), forward
    )
    intensity = 1.0 + jnp.sum(
        (far_field * far_field).reshape(position_count, mode_count * 2, length, length), axis=1
    )
    return jnp.sum((jnp.sqrt(intensity) - amplitude) ** 2)


def window_grads(windows, probe_modes, kernel, amplitude, forward, inverse):
    widened = windows.astype(jnp.float32)
    loss_value, pullback = jax.vjp(
        lambda window_f32: window_loss(
            window_f32, probe_modes, kernel, amplitude, forward, inverse
        ),
        widened,
    )
    return pullback(jnp.ones_like(loss_value))[0].astype(jnp.bfloat16)


def corner_index(row_start, col_start):
    zero_index = jnp.zeros((), jnp.int32)
    return (zero_index, zero_index, row_start, col_start)


def add_blocks(total, blocks, row_starts, col_starts):

    def add_one(item_index, running):
        item_index = item_index.astype(jnp.int32)
        block_f32 = blocks[item_index].astype(jnp.float32)
        corner = corner_index(row_starts[item_index], col_starts[item_index])
        current = lax.dynamic_slice(running, corner, block_f32.shape)
        return lax.dynamic_update_slice(running, current + block_f32, corner)

    return lax.fori_loop(0, blocks.shape[0], add_one, total)


def rank_within(owner_list):
    position_order = jnp.arange(owner_list.shape[0], dtype=jnp.int32)
    earlier = (owner_list[:, None] == owner_list[None, :]) & (
        position_order[:, None] > position_order[None, :]
    )
    return jnp.sum(earlier.astype(jnp.int32), axis=1)


def rows_from_pair(upper, lower, row_start, length):
    strip_rows = upper.shape[2]
    wanted_rows = row_start + jnp.arange(length, dtype=jnp.int32)
    from_upper = jnp.take(upper, jnp.clip(wanted_rows, 0, strip_rows - 1), axis=2)
    from_lower = jnp.take(lower, jnp.clip(wanted_rows - strip_rows, 0, strip_rows - 1), axis=2)
    return jnp.where((wanted_rows < strip_rows)[:, None], from_upper, from_lower)


def split_rows(grad_block, row_start, strip_rows):
    length = grad_block.shape[2]
    target_rows = jnp.arange(strip_rows, dtype=jnp.int32)
    upper_source = target_rows - row_start
    lower_source = upper_source + strip_rows
    upper_valid = (upper_source >= 0) & (upper_source < length)
    lower_valid = (lower_source >= 0) & (lower_source < length)
    upper_taken = jnp.take(grad_block, jnp.clip(upper_source, 0, length - 1), axis=2)
    lower_taken = jnp.take(grad_block, jnp.clip(lower_source, 0, length - 1), axis=2)
    zeros_like = jnp.zeros_like(upper_taken)
    return (
        jnp.where(upper_valid[:, None], upper_taken, zeros_like),
        jnp.where(lower_valid[:, None], lower_taken, zeros_like),
    )


def invert_slots(slot_index, slot_count):
    source_of = (
        jnp.zeros((slot_count,), jnp.int32)
        .at[slot_index]
        .set(jnp.arange(slot_index.shape[0], dtype=jnp.int32))
    )
    filled = jnp.zeros((slot_count,), jnp.int32).at[slot_index].set(1)
    return (source_of, filled > 0)


def per_device(object_field, probe_modes, propagator_phase, offsets, measured):
    devices_obj = lax.axis_size("obj")
    strip_rows = object_field.shape[2]
    length = probe_modes.shape[-1]
    position_count = offsets.shape[0]
    rounded = object_field.astype(jnp.bfloat16)
    top_strip = offsets[:, 0] // strip_rows
    row_within = offsets[:, 0] % strip_rows
    col_start = offsets[:, 1]
    forward = dft_blocks(length, 1.0)
    inverse = dft_blocks(length, -1.0)
    kernel = jnp.stack([jnp.cos(propagator_phase), jnp.sin(propagator_phase)])
    amplitude = jnp.sqrt(measured)
    owner_list = jnp.concatenate([top_strip, (top_strip + 1) % devices_obj])
    slot_index = owner_list * (2 * CAP) + rank_within(owner_list)
    slot_count = devices_obj * 2 * CAP
    request_table = (
        jnp.zeros((slot_count,), jnp.int32)
        .at[slot_index]
        .set(jnp.concatenate([col_start, col_start]))
    )
    wanted = lax.all_to_all(
        request_table.reshape(devices_obj, 2 * CAP), "obj", split_axis=0, concat_axis=0, tiled=True
    ).reshape(-1)
    outgoing = jax.vmap(
        lambda offset_col: lax.dynamic_slice_in_dim(rounded, offset_col, length, 3)
    )(wanted)
    block_shape = (devices_obj, 2 * CAP) + outgoing.shape[1:]
    arrived = lax.all_to_all(
        outgoing.reshape(block_shape), "obj", split_axis=0, concat_axis=0, tiled=True
    ).reshape(outgoing.shape)
    upper_blocks = arrived[slot_index[:position_count]]
    lower_blocks = arrived[slot_index[position_count:]]
    windows = jax.vmap(
        lambda upper, lower, offset_row: rows_from_pair(upper, lower, offset_row, length)
    )(upper_blocks, lower_blocks, row_within)
    window_grad = window_grads(windows, probe_modes, kernel, amplitude, forward, inverse)
    upper_grad, lower_grad = jax.vmap(
        lambda grad_block, offset_row: split_rows(grad_block, offset_row, strip_rows)
    )(window_grad, row_within)
    source_of, filled = invert_slots(slot_index, slot_count)
    item_of = source_of % position_count
    from_upper = (source_of < position_count)[:, None, None, None, None]
    chosen = jnp.where(from_upper, upper_grad[item_of], lower_grad[item_of])
    returning = jnp.where(filled[:, None, None, None, None], chosen, jnp.zeros_like(chosen))
    returned = lax.all_to_all(
        returning.reshape(block_shape), "obj", split_axis=0, concat_axis=0, tiled=True
    ).reshape(outgoing.shape)
    strip_grad = add_blocks(
        jnp.zeros(object_field.shape, jnp.float32), returned, jnp.zeros_like(wanted), wanted
    )
    return lax.psum_scatter(strip_grad, "pos", scatter_dimension=3, tiled=True)


def solution(mesh):
    placed = (
        P(None, None, "obj", None),
        P(),
        P(),
        P(("obj", "pos"), None),
        P(("obj", "pos"), None, None),
    )
    return jax.shard_map(
        per_device,
        mesh=mesh,
        in_specs=placed,
        out_specs=P(None, None, "obj", "pos"),
        check_vma=False,
    )
```

profile of v0, /device:TPU:1, one launch (start us, length us, event | category | flops | bytes accessed | tf_op | source)
XLA Modules:
  0.0 991.4 jit_solution(14176204370097873445)
XLA Ops:
  10.5 8.6 all-to-all-start
  19.1 5.4 copy.183
  25.5 19.0 %gather_fusion = bf16[64,2,2,128,128]{3,2,1,4,0:T(2,128)(2,1)} fusion(bf16[2,2,128,2048]{2,1,0,3:T(2,128)(2,1)S(1)} %copy.183, s32[64]{0:T(128)S(1)} %fusion.103), kind=kCustom, calls=%fused_computation.4 | custom fusion | bytes 16778240 | tf_op jit(solution)/shard_map/vmap()/gather | solution.py:156
  44.5 6.0 all-to-all-start.1
  57.7 130.8 %all-to-all-done.1 = bf16[16,4,2,2,128,128]{4,3,2,5,1,0:T(2,128)(2,1)} async-done(((bf16[16,4,2,2,128,128]{4,3,2,5,1,0:T(2,128)(2,1)}), bf16[16,4,2,2,128,128]{4,3,2,5,1,0:T(2,128)(2,1)}, u32[]{:S(2)}, u32[]{:S(2)}) %all-to-all-start.1) | async-done | bytes 8388640 | tf_op jit(solution)/shard_map/all_to_all | solution.py:159
  188.4 20.8 %copy.184 = bf16[16,4,2,2,128,128]{5,4,3,2,1,0:T(8,128)(2,1)} copy(bf16[16,4,2,2,128,128]{4,3,2,5,1,0:T(2,128)(2,1)} %all-to-all-done.1) | data formatting | bytes 16777216 | tf_op jit(solution)/shard_map/all_to_all | solution.py:159
  209.2 5.5 gather_fusion.1
  214.7 3.8 copy.185
  218.5 18.8 %gather_fusion.5 = bf16[2048,2,2,128]{3,2,1,0:T(2,128)(2,1)} fusion(bf16[16,2,2,128,128]{4,2,3,1,0:T(2,128)(2,1)S(1)} %copy.185, s32[2048]{0:T(1024)S(1)} %get-tuple-element.153), kind=kCustom, calls=%fused_computation.clone | custom fusion | bytes 4210688 | tf_op jit(solution)/shard_map/vmap(jit(_take))/gather | solution.py:100
  237.3 3.2 copy.186
  240.5 4.3 gather_fusion.2
  244.8 3.5 copy.187
  248.3 13.0 %gather_fusion.6 = bf16[2048,2,2,128]{3,2,1,0:T(2,128)(2,1)S(1)} fusion(bf16[16,2,2,128,128]{4,2,3,1,0:T(2,128)(2,1)} %copy.187, s32[2048]{0:T(1024)S(1)} %get-tuple-element.155), kind=kCustom, calls=%fused_computation.1.clone | custom fusion | bytes 4210688 | tf_op jit(solution)/shard_map/vmap(jit(_take))/gather | solution.py:101
  274.0 3.5 fusion
  277.4 3.8 fusion.29
  282.1 3.9 fusion.27
  286.0 5.6 fusion.16
  296.3 2.9 multiply_subtract_fusion
  299.3 3.5 fusion.3
  302.7 4.1 fusion.24
  308.9 7.1 fusion.22
  316.1 6.7 fusion.8
  322.8 3.1 fusion.38
  325.8 3.8 bitcast_multiply_fusion.5
  329.6 2.6 copy.209
  333.7 2.7 copy.212
  337.7 5.9 pad_add_fusion
  343.6 5.7 copy.214
  349.3 5.5 fusion.12
  354.8 7.2 fusion.32
  363.3 7.5 fusion.20
  370.8 7.4 fusion.6
  389.5 3.6 add_convert_fusion
  393.1 18.8 %gather_fusion.8 = bf16[2048,2,2,128]{3,2,1,0:T(2,128)(2,1)} fusion(bf16[16,2,2,128,128]{4,2,3,1,0:T(2,128)(2,1)S(1)} %add_convert_fusion, s32[2048]{0:T(1024)S(1)} %get-tuple-element.152), kind=kCustom, calls=%fused_computation.3.clone | custom fusion | bytes 4210688 | tf_op jit(solution)/shard_map/vmap(jit(_take))/gather | solution.py:113
  411.9 3.2 copy.230
  415.1 18.8 %gather_fusion.7 = bf16[2048,2,2,128]{3,2,1,0:T(2,128)(2,1)} fusion(bf16[16,2,2,128,128]{4,2,3,1,0:T(2,128)(2,1)S(1)} %add_convert_fusion, s32[2048]{0:T(1024)S(1)} %get-tuple-element.154), kind=kCustom, calls=%fused_computation.2.clone | custom fusion | bytes 4210688 | tf_op jit(solution)/shard_map/vmap(jit(_take))/gather | solution.py:112
  433.9 3.4 copy.229
  438.0 5.4 gather_fusion.4
  445.3 5.4 gather_fusion.3
  450.8 9.1 select_select_fusion
  459.9 8.6 all-to-all-start.2
  469.9 97.5 %all-to-all-done.2 = bf16[16,4,2,2,128,128]{5,4,3,2,1,0:T(8,128)(2,1)} async-done(((bf16[16,4,2,2,128,128]{5,4,3,2,1,0:T(8,128)(2,1)}), bf16[16,4,2,2,128,128]{5,4,3,2,1,0:T(8,128)(2,1)}, u32[]{:S(2)}, u32[]{:S(2)}) %all-to-all-start.2) | async-done | bytes 8388640 | tf_op jit(solution)/shard_map/all_to_all | solution.py:176
  569.9 355.0 %while.13 = (s32[]{:T(128)}, f32[2,2,128,2048]{3,2,1,0:T(8,128)}, s32[64]{0:T(128)S(1)}, bf16[64,2,2,128,128]{4,3,2,1,0:T(8,128)(2,1)}, s32[]{:T(128)}, /*index=5*/s32[]{:T(128)}, s32[]{:T(128)}) while((s32[]{:T(128)}, f32[2,2,128,2048]{3,2,1,0:T(8,128)}, s32[64]{0:T(128)S(1)}, bf16[64,2,2,128,128]{4,3,2,1,0:T(8,128)(2,1)}, s32[]{:T(128)}, ...), condition=%wide.region_15.17_spmd, body=%wide.region_14.16_spmd.sunk | while | flops 131077 | bytes 1179783 | solution.py:86
  748.8 2.6 dynamic_update_slice.8
  815.6 2.6 dynamic_update_slice.8
  860.0 2.6 dynamic_update_slice.8
  882.6 2.6 dynamic_update_slice.8
  924.9 59.5 %reduce-scatter.2.cloned.1.call-done = f32[2,2,128,256]{3,2,1,0:T(8,128)} async-done(((f32[2,2,128,2048]{3,2,1,0:T(8,128)}), f32[2,2,128,256]{3,2,1,0:T(8,128)}) %reduce-scatter.2.cloned.1.call-update) | async-done | bytes 524304 | tf_op jit(solution)/shard_map/reduce_scatter | solution.py:182
  (307 shorter events, 292.1 us)
Async XLA Ops:
  10.5 14.9 %all-to-all-start = ((s32[16,1,4]{2,1,0:T(1,128)}), s32[16,1,4]{2,1,0:T(1,128)S(1)}, u32[]{:S(2)}, u32[]{:S(2)}) async-start(s32[16,1,4]{2,1,0:T(1,128)} %bitcast.6), calls=%async_computation | async-start | bytes 16384 | tf_op jit(solution)/shard_map/all_to_all | solution.py:152
  44.5 6.0 copy-start.21
  44.5 6.3 copy-start.22
  44.5 143.9 %all-to-all-start.1 = ((bf16[16,4,2,2,128,128]{4,3,2,5,1,0:T(2,128)(2,1)}), bf16[16,4,2,2,128,128]{4,3,2,5,1,0:T(2,128)(2,1)}, u32[]{:S(2)}, u32[]{:S(2)}) async-start(bf16[16,4,2,2,128,128]{4,3,2,5,1,0:T(2,128)(2,1)} %bitcast.342), calls=%async_computation.1 | async-start | bytes 16777216 | tf_op jit(solution)/shard_map/all_to_all | solution.py:159
  50.5 1.3 copy-start.18
  50.7 221.0 %copy-start.12 = (f32[2,128,128]{1,2,0:T(8,128)}, f32[2,128,128]{1,2,0:T(8,128)S(1)}, u32[]{:S(2)}) copy-start(f32[2,128,128]{1,2,0:T(8,128)S(1)} %copy.182) | copy-start | bytes 393220
  50.8 220.9 %copy-start.14 = (f32[2,128,128]{1,2,0:T(8,128)}, f32[2,128,128]{1,2,0:T(8,128)S(1)}, u32[]{:S(2)}) copy-start(f32[2,128,128]{1,2,0:T(8,128)S(1)} %copy.190) | copy-start | bytes 393220
  51.9 229.4 %copy-start.19 = (f32[128,128]{0,1:T(8,128)}, f32[128,128]{0,1:T(8,128)S(1)}, u32[]{:S(2)}) copy-start(f32[128,128]{0,1:T(8,128)S(1)} %copy.195) | copy-start | bytes 196612
  261.4 1.6 copy-start.3
  306.8 1.2 copy-start.4
  316.1 6.7 copy-start
  329.6 2.6 copy-start.5
  333.7 4.0 copy-start.2
  343.6 5.7 copy-start.17
  349.3 5.5 copy-start.16
  354.8 7.2 copy-start.20
  370.8 7.4 copy-start.13
  370.8 7.4 copy-start.15
  383.7 2.7 copy-start.6
  385.1 1.4 copy-start.7
  386.4 2.0 copy-start.8
  386.4 2.2 copy-start.9
  386.4 2.5 copy-start.10
  386.5 2.8 copy-start.11
  433.9 3.4 copy-start.1
  459.9 107.5 %all-to-all-start.2 = ((bf16[16,4,2,2,128,128]{5,4,3,2,1,0:T(8,128)(2,1)}), bf16[16,4,2,2,128,128]{5,4,3,2,1,0:T(8,128)(2,1)}, u32[]{:S(2)}, u32[]{:S(2)}) async-start(bf16[16,4,2,2,128,128]{5,4,3,2,1,0:T(8,128)(2,1)} %select_select_fusion), calls=%async_computation.2 | async-start | bytes 16777216 | tf_op jit(solution)/shard_map/all_to_all | solution.py:176
  468.5 515.9 %reduce-scatter.2.cloned.1.call-start = ((), (), s32[]{:S(2)}) async-start(), calls=%async_computation.4 | async-start | bytes 4718592 | tf_op jit(solution)/shard_map/reduce_scatter | solution.py:182
Sparse Core Ops, SparseCore 0:
  925.0 59.3 reduce-scatter.1
where the time goes:
time: 1000 us; the launch traced here: 991 us
  local copies, waits for them, and re-layouts  368 us (37%)
  waiting for transfers between devices  289 us (29%)
  other arithmetic  125 us (12%)
  loops' own time  106 us (11%)
  matrix products  65.6 us (7%)
  starting transfers between devices  23.3 us (2%)
  between operations  14.2 us (1%)
    dynamic_update_slice x64, local copies, waits for them, and re-layouts, add_one(): return lax.dynamic_update_slice(running, current + block_f32, corner)  136 us
    all_to_all x1, waiting for transfers between devices, per_device(): lax.all_to_all(outgoing.reshape(block_shape), 'obj', split_axis=0, concat...  131 us
    another operation x1, loops' own time, add_blocks(): return lax.fori_loop(0, blocks.shape[0], add_one, total)  106 us
    all_to_all x1, waiting for transfers between devices, per_device(): lax.all_to_all(returning.reshape(block_shape), 'obj', split_axis=0, conca...  97.5 us
    add x64, other arithmetic, add_one(): return lax.dynamic_update_slice(running, current + block_f32, corner)  77.1 us
    reduce_scatter x1, waiting for transfers between devices, per_device(): return lax.psum_scatter(strip_grad, 'pos', scatter_dimension=3, tiled=True)  59.5 us
    dynamic_slice x64, local copies, waits for them, and re-layouts, add_one(): corner = corner_index(row_starts[item_index], col_starts[item_index])  35.5 us
    dot_general x6, matrix products, transform(): jnp.einsum('naik,cakl->ncil', rows_done, blocks, precision=lax.Precision....  33.6 us
  transfers between devices with their start and end apart: 4, of which 4 were waited for; matrix products, arithmetic and copies ran while one was open for 1% of the time, Pallas kernels for 0%

commit v1 on v0

v1 whole, which is shorter than its diff:
```python
import functools
import math

import jax
import jax.numpy as jnp
import numpy as np
from jax import lax
from jax.experimental import pallas as pl
from jax.experimental.pallas import tpu as pltpu
from jax.sharding import PartitionSpec as P

CAP = 2
SIDE = 128
AMP = jnp.int16
AMP_MIDDLE, AMP_STEPS = 2.625, 16384.0
MESH = pl.DeviceIdType.MESH


def dft_operands():
    index = np.arange(SIDE)
    angles = (index[:, None] * index[None, :] % SIDE) * (2.0 * math.pi / SIDE)
    cosine = np.cos(angles) / math.sqrt(SIDE)
    sine = np.sin(angles) / math.sqrt(SIDE)

    def parts(block, axis):
        block = block.astype(np.float32)
        high = block.astype(jnp.bfloat16)
        low = (block - high.astype(np.float32)).astype(jnp.bfloat16)
        return np.concatenate([high, low, high], axis=axis)

    left, right = [], []
    for sign in (1.0, -1.0):
        s = sign * sine
        left.append(parts(np.block([[cosine, s], [-s, cosine]]), 1))
        right.append(parts(np.block([[cosine, -s], [s, cosine]]), 0))
    return np.stack(left), np.stack(right)


def coded(measured):
    return jnp.round((jnp.sqrt(measured) - AMP_MIDDLE) * AMP_STEPS).astype(jnp.int32).astype(AMP)


def decoded(code):
    return code.astype(jnp.int32).astype(jnp.float32) * (1.0 / AMP_STEPS) + AMP_MIDDLE


def split3(x, axis):
    high = x.astype(jnp.bfloat16)
    low = (x - high.astype(jnp.float32)).astype(jnp.bfloat16)
    return jnp.concatenate([high, high, low], axis=axis)


def transform2d(left, right, real, imag):
    fields = real.shape[1] // SIDE
    y = jnp.dot(left, split3(jnp.concatenate([real, imag], axis=0), 0), preferred_element_type=jnp.float32)
    rows = [
        jnp.concatenate([y[:SIDE, k * SIDE : (k + 1) * SIDE], y[SIDE:, k * SIDE : (k + 1) * SIDE]], axis=1)
        for k in range(fields)
    ]
    z = jnp.dot(split3(jnp.concatenate(rows, axis=0), 1), right, preferred_element_type=jnp.float32)
    out_real = jnp.concatenate([z[k * SIDE : (k + 1) * SIDE, :SIDE] for k in range(fields)], axis=1)
    out_imag = jnp.concatenate([z[k * SIDE : (k + 1) * SIDE, SIDE:] for k in range(fields)], axis=1)
    return out_real, out_imag


def grads_kernel(batch, own_ref, halo_ref, amp_ref, meta_ref, probe_ref, prop_ref, left_ref, right_ref, grad_ref, field, order):
    fields = 2 * batch

    def widen(index, _):
        plane, block = index // 16, index % 16
        columns = pl.ds(pl.multiple_of(block * SIDE, SIDE), SIDE)
        field[plane, block, :SIDE, :] = own_ref[plane, :, columns].astype(jnp.bfloat16).astype(jnp.float32)
        field[plane, block, SIDE:, :] = halo_ref[block // 2, plane, block % 2].astype(jnp.float32)
        grad_ref[plane, block] = jnp.zeros((2 * SIDE, SIDE), jnp.float32)
        return 0

    lax.fori_loop(0, 64, widen, 0)

    def collect(slot, count):
        order[count] = slot
        return count + (meta_ref[slot // 2, 0, slot % 2] > 0).astype(jnp.int32)

    count = lax.fori_loop(0, 32, collect, 0)
    lane = lax.broadcasted_iota(jnp.int32, (SIDE, SIDE), 1)

    def place(slot):
        code = jnp.maximum(meta_ref[slot // 2, 0, slot % 2] - 1, 0)
        row, col = code // 2048, code % 2048
        block, shift = col // SIDE, col % SIDE
        return pl.ds(row, SIDE), block, jnp.minimum(block + 1, 15), shift

    def cut(plane, where):
        rows, block, next_block, shift = where
        back = (SIDE - shift) % SIDE
        first = pltpu.roll(field[plane, block, rows, :], back, 1)
        second = pltpu.roll(field[plane, next_block, rows, :], back, 1)
        return jnp.where(lane < SIDE - shift, first, second)

    def add(plane, where, value):
        rows, block, next_block, shift = where
        moved = pltpu.roll(value.astype(jnp.bfloat16).astype(jnp.float32), shift, 1)
        zero = jnp.zeros_like(moved)
        grad_ref[plane, block, rows, :] += jnp.where(lane >= shift, moved, zero)
        grad_ref[plane, next_block, rows, :] += jnp.where(lane < shift, moved, zero)

    def side_by_side(parts):
        return jnp.concatenate(parts, axis=1)

    def step(index, _):
        slots, wheres, weights = [], [], []
        for k in range(batch):
            item = index * batch + k
            slot = order[jnp.minimum(item, count - 1)]
            slots.append(slot)
            wheres.append(place(slot))
            weights.append(jnp.where(item < count, 2.0, 0.0).astype(jnp.float32))
        t = [[cut(plane, where) for where in wheres] for plane in range(4)]
        t0r, t1r, t0i, t1i = [side_by_side([x for x in plane for _ in range(2)]) for plane in t]
        pr = side_by_side([probe_ref[0, 0], probe_ref[1, 0]] * batch)
        pi = side_by_side([probe_ref[0, 1], probe_ref[1, 1]] * batch)
        kr = side_by_side([prop_ref[0]] * fields)
        ki = side_by_side([prop_ref[1]] * fields)
        forward = (left_ref[0], right_ref[0])
        inverse = (left_ref[1], right_ref[1])
        wr, wi = pr * t0r - pi * t0i, pr * t0i + pi * t0r
        sr, si = transform2d(*forward, wr, wi)
        ur, ui = transform2d(*inverse, sr * kr - si * ki, sr * ki + si * kr)
        fr, fi = transform2d(*forward, ur * t1r - ui * t1i, ur * t1i + ui * t1r)
        power = fr * fr + fi * fi
        factors = []
        for k in range(batch):
            low = 2 * k * SIDE
            model = 1.0 + power[:, low : low + SIDE] + power[:, low + SIDE : low + 2 * SIDE]
            amplitude = decoded(amp_ref[slots[k]])
            factors += [weights[k] * (1.0 - amplitude * lax.rsqrt(model))] * 2
        q = side_by_side(factors)
        gr, gi = transform2d(*inverse, fr * q, fi * q)
        d1r, d1i = ur * gr + ui * gi, ur * gi - ui * gr
        hr, hi = transform2d(*forward, t1r * gr + t1i * gi, t1r * gi - t1i * gr)
        er, ei = transform2d(*inverse, kr * hr + ki * hi, kr * hi - ki * hr)
        d0r, d0i = pr * er + pi * ei, pr * ei - pi * er
        for k in range(batch):
            low = 2 * k * SIDE
            for plane, value in enumerate((d0r, d1r, d0i, d1i)):
                add(plane, wheres[k], value[:, low : low + SIDE] + value[:, low + SIDE : low + 2 * SIDE])
        return 0

    lax.fori_loop(0, (count + batch - 1) // batch, step, 0)


def grads_call(own, halo, amp, meta, probe, prop, batch=1):
    left, right = dft_operands()
    vmem = pl.BlockSpec(memory_space=pltpu.VMEM)
    return pl.pallas_call(
        functools.partial(grads_kernel, batch),
        out_shape=jax.ShapeDtypeStruct((4, 16, 2 * SIDE, SIDE), jnp.float32),
        in_specs=[vmem, vmem, vmem, pl.BlockSpec(memory_space=pltpu.SMEM)] + [vmem] * 4,
        out_specs=vmem,
        scratch_shapes=[pltpu.VMEM((4, 16, 2 * SIDE, SIDE), jnp.float32), pltpu.SMEM((33,), jnp.int32)],
        compiler_params=pltpu.CompilerParams(vmem_limit_bytes=56 * 2**20),
        name="window_gradients",
    )(own, halo, amp, meta, probe, prop, jnp.asarray(left), jnp.asarray(right))


def send_kernel(obj_ref, measured_ref, source_ref, code_ref, halo_ref, amp_ref, meta_ref, wide, chunk, amp_out, meta_out, local_sem, halo_send, halo_recv, amp_send, amp_recv, meta_send, meta_recv):
    strip, pos = lax.axis_index("obj"), lax.axis_index("pos")
    x, core = pos // 2, pos % 2
    load = pltpu.make_async_copy(obj_ref.at[:, :, pl.ds(pl.multiple_of(pos * 256, 256), 256)], wide, local_sem.at[0])
    load.start()
    barrier = pltpu.get_barrier_semaphore()

    def greet_strip(step, _):
        pl.semaphore_signal(barrier, inc=1, device_id=(lax.rem(strip + step, 16), pos), device_id_type=MESH)
        return 0

    lax.fori_loop(1, 16, greet_strip, 0)
    for step in range(1, 4):
        other = lax.rem(x + step, 4) * 2 + core
        pl.semaphore_signal(barrier, inc=1, device_id=(strip, other), device_id_type=MESH)
    twin = x * 2 + 1 - core
    pl.semaphore_signal(barrier, inc=1, device_id=(strip, twin), device_id_type=MESH)
    load.wait()
    for block in range(2):
        chunk[:, block] = wide[:, :, block * SIDE : (block + 1) * SIDE].astype(jnp.bfloat16)
    pl.semaphore_wait(barrier, 19)

    def forward_chunk(source, index, where, send):
        return pltpu.make_async_remote_copy(
            src_ref=source, dst_ref=halo_ref.at[index], send_sem=halo_send.at[send], recv_sem=halo_recv.at[index],
            device_id=where, device_id_type=MESH,
        )

    first = forward_chunk(chunk, pos, (lax.rem(strip + 15, 16), pos), 0)
    first.start()

    def amp_copy(target):
        return pltpu.make_async_remote_copy(
            src_ref=amp_out.at[target], dst_ref=amp_ref.at[strip], send_sem=amp_send.at[target], recv_sem=amp_recv.at[strip],
            device_id=(target, pos), device_id_type=MESH,
        )

    def meta_copy(target):
        return pltpu.make_async_remote_copy(
            src_ref=meta_out.at[target], dst_ref=meta_ref.at[strip], send_sem=meta_send.at[target], recv_sem=meta_recv.at[strip],
            device_id=(target, pos), device_id_type=MESH,
        )

    lane = lax.broadcasted_iota(jnp.int32, (8, SIDE), 1)

    def packed(target):
        codes = jnp.where(lane == 0, code_ref[2 * target], code_ref[2 * target + 1])
        values = [coded(measured_ref[source_ref[2 * target + k]]) for k in range(CAP)]
        return codes, values

    def pack(step, _):
        target = lax.rem(strip + step, 16)
        codes, values = packed(target)
        meta_out[target] = codes
        for k in range(CAP):
            amp_out[target, k] = values[k]
        amp_copy(target).start()
        meta_copy(target).start()
        return 0

    lax.fori_loop(1, 16, pack, 0)
    codes, values = packed(strip)
    meta_ref[strip] = codes
    for k in range(CAP):
        amp_ref[strip, k] = values[k]

    first.wait_recv()
    sends = [first]
    for step in (2, 1, 3):
        copy = forward_chunk(halo_ref.at[pos], pos, (strip, lax.rem(x + step, 4) * 2 + core), step)
        copy.start()
        sends.append(copy)
    copy = forward_chunk(halo_ref.at[pos], pos, (strip, twin), 4)
    copy.start()
    sends.append(copy)
    for step in (1, 3, 2):
        index = lax.rem(x + step, 4) * 2 + core
        forward_chunk(chunk, index, (strip, twin), 0).wait_recv()
        copy = forward_chunk(halo_ref.at[index], index, (strip, twin), 4 + step)
        copy.start()
        sends.append(copy)
    for step in range(4):
        index = lax.rem(x + step, 4) * 2 + 1 - core
        forward_chunk(chunk, index, (strip, twin), 0).wait_recv()

    def finish(step, _):
        target = lax.rem(strip + step, 16)
        source = lax.rem(strip + 16 - step, 16)
        amp_copy(target).wait_send()
        meta_copy(target).wait_send()
        pltpu.make_async_remote_copy(
            src_ref=amp_out.at[target], dst_ref=amp_ref.at[source], send_sem=amp_send.at[target], recv_sem=amp_recv.at[source],
            device_id=(target, pos), device_id_type=MESH,
        ).wait_recv()
        pltpu.make_async_remote_copy(
            src_ref=meta_out.at[target], dst_ref=meta_ref.at[source], send_sem=meta_send.at[target], recv_sem=meta_recv.at[source],
            device_id=(target, pos), device_id_type=MESH,
        ).wait_recv()
        return 0

    lax.fori_loop(1, 16, finish, 0)
    for copy in sends:
        copy.wait_send()


def send_call(obj, measured, source, code):
    vmem = pl.BlockSpec(memory_space=pltpu.VMEM)
    smem = pl.BlockSpec(memory_space=pltpu.SMEM)
    dma = pltpu.SemaphoreType.DMA
    return pl.pallas_call(
        send_kernel,
        out_shape=(
            jax.ShapeDtypeStruct((8, 4, 2, SIDE, SIDE), jnp.bfloat16),
            jax.ShapeDtypeStruct((16, CAP, SIDE, SIDE), AMP),
            jax.ShapeDtypeStruct((16, 8, SIDE), jnp.int32),
        ),
        in_specs=[pl.BlockSpec(memory_space=pl.ANY), vmem, smem, smem],
        out_specs=(vmem, vmem, vmem),
        scratch_shapes=[
            pltpu.VMEM((4, SIDE, 256), jnp.float32),
            pltpu.VMEM((4, 2, SIDE, SIDE), jnp.bfloat16),
            pltpu.VMEM((16, CAP, SIDE, SIDE), AMP),
            pltpu.VMEM((16, 8, SIDE), jnp.int32),
            dma((1,)),
            dma((8,)),
            dma((8,)),
            dma((16,)),
            dma((16,)),
            dma((16,)),
            dma((16,)),
        ],
        compiler_params=pltpu.CompilerParams(collective_id=0, has_side_effects=True, vmem_limit_bytes=32 * 2**20),
        name="exchange_inputs",
    )(obj, measured, source, code)


def sum_kernel(grad_ref, out_ref, half, summed, parts, low_in, low_out, total, twin_send, twin_recv, x_send, x_recv, low_send, low_recv):
    strip, pos = lax.axis_index("obj"), lax.axis_index("pos")
    x, core = pos // 2, pos % 2
    twin = (strip, x * 2 + 1 - core)
    below, above = (lax.rem(strip + 1, 16), pos), (lax.rem(strip + 15, 16), pos)
    barrier = pltpu.get_barrier_semaphore()
    peers = [(strip, lax.rem(x + step, 4) * 2 + core) for step in range(4)]
    for device in (twin, below, above, *peers[1:]):
        pl.semaphore_signal(barrier, inc=1, device_id=device, device_id_type=MESH)
    pl.semaphore_wait(barrier, 6)

    def columns(step, side):
        return pl.ds(lax.rem(x + step, 4) * 4 + 2 * side, 2)

    steps = (2, 1, 3, 0)
    twin_copies = {}
    for step in steps:
        copy = pltpu.make_async_remote_copy(
            src_ref=grad_ref.at[:, columns(step, 1 - core)], dst_ref=half.at[step], send_sem=twin_send.at[step],
            recv_sem=twin_recv.at[step], device_id=twin, device_id_type=MESH,
        )
        copy.start()
        twin_copies[step] = copy
    x_copies = {}
    for step in steps:
        twin_copies[step].wait_recv()
        first = lax.rem(x + step, 4) * 4 + 2 * core
        if step:
            for plane in range(4):
                for block in range(2):
                    summed[step - 1, plane, block] = (grad_ref[plane, first + block] + half[step, plane, block]).astype(jnp.bfloat16)
            copy = pltpu.make_async_remote_copy(
                src_ref=summed.at[step - 1], dst_ref=parts.at[step - 1], send_sem=x_send.at[step - 1],
                recv_sem=x_recv.at[step - 1], device_id=peers[step], device_id_type=MESH,
            )
            copy.start()
            x_copies[step] = copy
        else:
            for plane in range(4):
                for block in range(2):
                    total[plane, block] = grad_ref[plane, first + block] + half[step, plane, block]
    for step in (1, 3, 2):
        x_copies[step].wait_recv()
    for plane in range(4):
        for block in range(2):
            value = total[plane, block, SIDE:]
            for step in range(3):
                value += parts[step, plane, block, SIDE:].astype(jnp.float32)
            low_out[plane, block] = value.astype(jnp.bfloat16)
    copy = pltpu.make_async_remote_copy(
        src_ref=low_out, dst_ref=low_in, send_sem=low_send, recv_sem=low_recv, device_id=below, device_id_type=MESH,
    )
    copy.start()
    for plane in range(4):
        for block in range(2):
            value = total[plane, block, :SIDE]
            for step in range(3):
                value += parts[step, plane, block, :SIDE].astype(jnp.float32)
            total[plane, block, :SIDE] = value
    copy.wait_recv()
    for plane in range(4):
        for block in range(2):
            out_ref[plane, :, block * SIDE : (block + 1) * SIDE] = total[plane, block, :SIDE] + low_in[plane, block].astype(jnp.float32)
    copy.wait_send()
    for step in steps:
        twin_copies[step].wait_send()
    for step in (1, 2, 3):
        x_copies[step].wait_send()


def sum_call(grad):
    vmem = pl.BlockSpec(memory_space=pltpu.VMEM)
    dma = pltpu.SemaphoreType.DMA
    return pl.pallas_call(
        sum_kernel,
        out_shape=jax.ShapeDtypeStruct((4, SIDE, 256), jnp.float32),
        in_specs=[vmem],
        out_specs=vmem,
        scratch_shapes=[
            pltpu.VMEM((4, 4, 2, 2 * SIDE, SIDE), jnp.float32),
            pltpu.VMEM((3, 4, 2, 2 * SIDE, SIDE), jnp.bfloat16),
            pltpu.VMEM((3, 4, 2, 2 * SIDE, SIDE), jnp.bfloat16),
            pltpu.VMEM((4, 2, SIDE, SIDE), jnp.bfloat16),
            pltpu.VMEM((4, 2, SIDE, SIDE), jnp.bfloat16),
            pltpu.VMEM((4, 2, 2 * SIDE, SIDE), jnp.float32),
            dma((4,)),
            dma((4,)),
            dma((3,)),
            dma((3,)),
            dma,
            dma,
        ],
        compiler_params=pltpu.CompilerParams(collective_id=1, has_side_effects=True, vmem_limit_bytes=32 * 2**20),
        name="sum_gradients",
    )(grad)


def per_device(object_field, probe_modes, propagator_phase, offsets, measured):
    obj = object_field.reshape(4, SIDE, object_field.shape[3])
    position = jnp.arange(offsets.shape[0], dtype=jnp.int32)
    top = offsets[:, 0] // SIDE
    earlier = (top[:, None] == top[None, :]) & (position[:, None] > position[None, :])
    slot = top * CAP + jnp.sum(earlier.astype(jnp.int32), axis=1)
    chosen = (slot[None, :] == jnp.arange(16 * CAP, dtype=jnp.int32)[:, None]).astype(jnp.int32)
    source = jnp.sum(chosen * position[None, :], axis=1)
    code = jnp.sum(chosen * (1 + (offsets[:, 0] % SIDE) * 2048 + offsets[:, 1])[None, :], axis=1)
    prop = jnp.stack([jnp.cos(propagator_phase), jnp.sin(propagator_phase)])
    halo, amp, meta = send_call(obj, measured, source, code)
    grad = grads_call(obj, halo, amp.reshape(16 * CAP, SIDE, SIDE), meta, probe_modes, prop)
    return sum_call(grad).reshape(2, 2, SIDE, 256)


def solution(mesh):
    placed = (
        P(None, None, "obj", None),
        P(),
        P(),
        P(("obj", "pos"), None),
        P(("obj", "pos"), None, None),
    )
    return jax.shard_map(
        per_device,
        mesh=mesh,
        in_specs=placed,
        out_specs=P(None, None, "obj", "pos"),
        check_vma=False,
    )
```

time: 1000 us -> 194 us (0.19)
  the two profiles are of different devices: /device:TPU:1 before, /device:TPU:6 now
where the time goes in v1:
time: 194 us
  Pallas kernels  179 us (92%)
  local copies, waits for them, and re-layouts  11.6 us (6%)
  other arithmetic  3 us (2%)
    pallas_call x1, Pallas kernels, grads_call(): pl.pallas_call(functools.partial(grads_kernel, batch), out_shape=jax.Shap...  78.1 us
    pallas_call x1, Pallas kernels, sum_call(): pl.pallas_call(sum_kernel, out_shape=jax.ShapeDtypeStruct((4, SIDE, 256),...  63.7 us
    pallas_call x1, Pallas kernels, send_call(): pl.pallas_call(send_kernel, out_shape=(jax.ShapeDtypeStruct((8, 4, 2, SID...  37.4 us
    unnamed x13, local copies, waits for them, and re-layouts  10.5 us

profile of v1, /device:TPU:6, one launch (start us, length us, event | category | flops | bytes accessed | tf_op | source)
XLA Modules:
  0.0 193.8 jit_solution(3878848344211191535)
XLA Ops:
  0.0 0.7 fusion.4
  0.7 0.7 and_select_fusion.2
  1.4 0.2 convert_reduce_fusion
  1.6 0.7 fusion.3
  2.2 0.1 select_reduce_fusion
  2.3 1.1 cosine_bitcast_fusion
  3.4 0.7 pad_maximum_fusion.prop_ref
  4.1 0.0 copy-start.1
  4.1 2.2 %copy-done.1 = f32[2,2,128,2048]{3,2,1,0:T(8,128)S(1)} copy-done((f32[2,2,128,2048]{3,2,1,0:T(8,128)S(1)}, f32[2,2,128,2048]{3,2,1,0:T(8,128)}, u32[]{:S(2)}) %copy-start.1) | copy-done | bytes 4194328
  6.3 0.0 copy-start.4
  6.3 1.2 copy-done.4
  7.5 37.4 %exchange_inputs.1 = (bf16[8,4,2,128,128]{4,3,2,1,0:T(8,128)(2,1)S(1)}, s16[16,2,128,128]{3,2,1,0:T(8,128)(2,1)S(1)}, s32[16,8,128]{2,1,0:T(8,128)S(1)}) custom-call(f32[4,128,2048]{2,1,0:T(8,128)S(1)} %bitcast.24, f32[16,128,128]{2,1,0:T(8,128)S(1)} %copy-done.4, s32[32]{0:T(128)S(1)} %get-tuple-element.12.source_ref, s32[32]{0:T(128)S(1)} %get-tuple-element.11.code_ref), custom_call_target="tpu_custom_call" | custom-call | tf_op jit(solution)/shard_map/exchange_inputs/pallas_call | solution.py:274
  44.9 0.0 copy-start.2
  44.9 1.4 copy-done.2
  46.3 0.0 copy-start.3
  46.3 1.0 copy-done.3
  47.2 0.0 copy-start.5
  47.2 0.6 copy-done.5
  47.9 78.1 %window_gradients.1.grad_ref = f32[4,16,256,128]{3,2,1,0:T(8,128)} custom-call(f32[4,128,2048]{2,1,0:T(8,128)} %bitcast.23, bf16[8,4,2,128,128]{4,3,2,1,0:T(8,128)(2,1)} %copy-done.2, s16[32,128,128]{2,1,0:T(8,128)(2,1)} %bitcast.26, s32[16,8,128]{2,1,0:T(8,128)} %copy-done.5, f32[2,2,128,128]{3,2,1,0:T(8,128)} %probe_ref.1, ...), custom_call_target="tpu_custom_call" | custom-call | tf_op jit(solution)/shard_map/window_gradients/pallas_call | solution.py:154
  125.9 0.0 copy-start
  125.9 3.4 %copy-done = f32[4,16,256,128]{3,2,1,0:T(8,128)S(1)} copy-done((f32[4,16,256,128]{3,2,1,0:T(8,128)S(1)}, f32[4,16,256,128]{3,2,1,0:T(8,128)}, u32[]{:S(2)}) %copy-start) | copy-done | bytes 8388632
  129.3 63.7 %sum_gradients.1 = f32[4,128,256]{2,1,0:T(8,128)S(1)} custom-call(f32[4,16,256,128]{3,2,1,0:T(8,128)S(1)} %copy-done), custom_call_target="tpu_custom_call" | custom-call | tf_op jit(solution)/shard_map/sum_gradients/pallas_call | solution.py:374
  193.0 0.8 copy.9
Async XLA Ops:
  4.1 2.2 %copy-start.1 = (f32[2,2,128,2048]{3,2,1,0:T(8,128)S(1)}, f32[2,2,128,2048]{3,2,1,0:T(8,128)}, u32[]{:S(2)}) copy-start(f32[2,2,128,2048]{3,2,1,0:T(8,128)} %param.7) | copy-start | bytes 12582916
  6.3 1.2 copy-start.4
  44.9 1.4 copy-start.2
  46.3 1.0 copy-start.3
  47.2 0.6 copy-start.5
  125.9 3.4 %copy-start = (f32[4,16,256,128]{3,2,1,0:T(8,128)S(1)}, f32[4,16,256,128]{3,2,1,0:T(8,128)}, u32[]{:S(2)}) copy-start(f32[4,16,256,128]{3,2,1,0:T(8,128)} %window_gradients.1.grad_ref) | copy-start | bytes 25165828

commit v2 on v1

v2 whole, which is shorter than its diff:
```python
import functools
import math

import jax
import jax.numpy as jnp
import numpy as np
from jax import lax
from jax.experimental import pallas as pl
from jax.experimental.pallas import tpu as pltpu
from jax.sharding import PartitionSpec as P

CAP = 2
SIDE = 128
SPAN = 10
LOW_COL, HIGH_COL = 768, 1152
AMP = jnp.int16
AMP_MIDDLE, AMP_STEPS = 2.625, 16384.0
MESH = pl.DeviceIdType.MESH


def dft_operands():
    index = np.arange(SIDE)
    angles = (index[:, None] * index[None, :] % SIDE) * (2.0 * math.pi / SIDE)
    cosine = np.cos(angles) / math.sqrt(SIDE)
    sine = np.sin(angles) / math.sqrt(SIDE)

    def parts(block, axis):
        block = block.astype(np.float32)
        high = block.astype(jnp.bfloat16)
        low = (block - high.astype(np.float32)).astype(jnp.bfloat16)
        return np.concatenate([high, low, high], axis=axis)

    left, right = [], []
    for sign in (1.0, -1.0):
        s = sign * sine
        left.append(parts(np.block([[cosine, s], [-s, cosine]]), 1))
        right.append(parts(np.block([[cosine, -s], [s, cosine]]), 0))
    return np.stack(left), np.stack(right)


def coded(measured):
    return jnp.round((jnp.sqrt(measured) - AMP_MIDDLE) * AMP_STEPS).astype(jnp.int32).astype(AMP)


def decoded(code):
    return code.astype(jnp.int32).astype(jnp.float32) * (1.0 / AMP_STEPS) + AMP_MIDDLE


def split3(x, axis):
    high = x.astype(jnp.bfloat16)
    low = (x - high.astype(jnp.float32)).astype(jnp.bfloat16)
    return jnp.concatenate([high, high, low], axis=axis)


def transform2d(left, right, which, real, imag):
    fields = real.shape[1] // SIDE
    y = jnp.dot(left[which], split3(jnp.concatenate([real, imag], axis=0), 0), preferred_element_type=jnp.float32)
    yield
    rows = [
        jnp.concatenate([y[:SIDE, k * SIDE : (k + 1) * SIDE], y[SIDE:, k * SIDE : (k + 1) * SIDE]], axis=1)
        for k in range(fields)
    ]
    z = jnp.dot(split3(jnp.concatenate(rows, axis=0), 1), right[which], preferred_element_type=jnp.float32)
    yield
    out_real = jnp.concatenate([z[k * SIDE : (k + 1) * SIDE, :SIDE] for k in range(fields)], axis=1)
    out_imag = jnp.concatenate([z[k * SIDE : (k + 1) * SIDE, SIDE:] for k in range(fields)], axis=1)
    return out_real, out_imag


def grads_kernel(obj_ref, halo_ref, amp_hbm, meta_ref, probe_hbm, phase_hbm, left_hbm, right_hbm, grad_hbm,
                 field, grad, own, halo, amp, probe, phase, left_ref, right_ref, prop_ref, packed, order, sems, out_sem):
    core = lax.axis_index("pos") % 2
    base = 6 * core
    columns = pl.ds(pl.multiple_of(base * SIDE, SIDE), SPAN * SIDE)
    loads = [
        pltpu.make_async_copy(source, target, sems.at[k])
        for k, (source, target) in enumerate([
            (obj_ref.at[:, :, columns], own),
            (halo_ref, halo),
            (phase_hbm, phase),
            (probe_hbm, probe),
            (left_hbm, left_ref),
            (right_hbm, right_ref),
            (amp_hbm, amp),
        ])
    ]
    for load in loads:
        load.start()

    def read(slot):
        code = meta_ref[slot // 32, slot % 32 // 2, 0, slot % 2] - 1
        return code >= 0, code // 2048, code % 2048

    def tally(slot, counts):
        valid, _, col = read(slot)
        here = valid.astype(jnp.int32)
        first = here * (col < LOW_COL).astype(jnp.int32)
        last = here * (col > HIGH_COL).astype(jnp.int32)
        return counts[0] + here, counts[1] + first, counts[2] + last

    whole, first_only, last_only = lax.fori_loop(0, 64, tally, (0, 0, 0))
    either = whole - first_only - last_only
    to_first = jnp.clip((whole + 1) // 2 - first_only, 0, either)

    def collect(slot, state):
        count, seen = state
        valid, _, col = read(slot)
        free = (col >= LOW_COL) & (col <= HIGH_COL)
        on_first = (col < LOW_COL) | (free & (seen < to_first))
        order[count] = slot
        mine = valid & (on_first == (core == 0))
        return count + mine.astype(jnp.int32), seen + (valid & free).astype(jnp.int32)

    count, _ = lax.fori_loop(0, 64, collect, (0, 0))
    loads[0].wait()
    loads[1].wait()

    def widen(index, _):
        plane, block = index // SPAN, index % SPAN
        inside = block + base - 8 * core
        within = (inside >= 0) & (inside < 8)
        extra = block + base - (8 - 2 * core)
        part = jnp.where(within, inside // 2, plane)
        tile = jnp.where(within, plane * 2 + inside % 2, 8 + extra)
        span = pl.ds(pl.multiple_of(block * SIDE, SIDE), SIDE)
        field[plane, block, :SIDE, :] = own[plane, :, span].astype(jnp.bfloat16).astype(jnp.float32)
        field[plane, block, SIDE:, :] = halo[part, tile].astype(jnp.float32)
        grad[block, plane] = jnp.zeros((2 * SIDE, SIDE), jnp.float32)
        return 0

    lax.fori_loop(0, 4 * SPAN, widen, 0)
    loads[2].wait()
    prop_ref[0] = jnp.cos(phase[...])
    prop_ref[1] = jnp.sin(phase[...])
    for load in loads[3:]:
        load.wait()
    lane = lax.broadcasted_iota(jnp.int32, (SIDE, SIDE), 1)

    def place(slot):
        valid, row, col = read(slot)
        row, col = jnp.where(valid, row, 0), jnp.where(valid, col, base * SIDE)
        block, shift = jnp.clip(col // SIDE - base, 0, SPAN - 1), col % SIDE
        return pl.ds(row, SIDE), block, jnp.minimum(block + 1, SPAN - 1), shift

    def cut(plane, where):
        rows, block, next_block, shift = where
        back = (SIDE - shift) % SIDE
        first = pltpu.roll(field[plane, block, rows, :], back, 1)
        second = pltpu.roll(field[plane, next_block, rows, :], back, 1)
        return jnp.where(lane < SIDE - shift, first, second)

    def add(plane, where, value):
        rows, block, next_block, shift = where
        moved = pltpu.roll(value.astype(jnp.bfloat16).astype(jnp.float32), shift, 1)
        zero = jnp.zeros_like(moved)
        grad[block, plane, rows, :] += jnp.where(lane >= shift, moved, zero)
        grad[next_block, plane, rows, :] += jnp.where(lane < shift, moved, zero)

    def pair(parts):
        return jnp.concatenate(parts, axis=1)

    forward = (left_ref, right_ref, 0)
    inverse = (left_ref, right_ref, 1)

    def stages(where, slot, weight):
        t0r, t1r, t0i, t1i = [pair([cut(plane, where)] * 2) for plane in range(4)]
        pr, pi = [pair([probe[0, k], probe[1, k]]) for k in range(2)]
        kr, ki = [pair([prop_ref[k]] * 2) for k in range(2)]
        wr, wi = pr * t0r - pi * t0i, pr * t0i + pi * t0r
        yield
        sr, si = yield from transform2d(*forward, wr, wi)
        ur, ui = yield from transform2d(*inverse, sr * kr - si * ki, sr * ki + si * kr)
        fr, fi = yield from transform2d(*forward, ur * t1r - ui * t1i, ur * t1i + ui * t1r)
        power = fr * fr + fi * fi
        model = 1.0 + power[:, :SIDE] + power[:, SIDE:]
        amplitude = decoded(amp[slot // 32, slot % 32 // 2, slot % 2])
        factor = pair([weight * (1.0 - amplitude * lax.rsqrt(model))] * 2)
        gr, gi = yield from transform2d(*inverse, fr * factor, fi * factor)
        for plane, value in ((1, ur * gr + ui * gi), (3, ur * gi - ui * gr)):
            add(plane, where, value[:, :SIDE] + value[:, SIDE:])
        hr, hi = yield from transform2d(*forward, t1r * gr + t1i * gi, t1r * gi - t1i * gr)
        er, ei = yield from transform2d(*inverse, kr * hr + ki * hi, kr * hi - ki * hr)
        for plane, value in ((0, pr * er + pi * ei), (2, pr * ei - pi * er)):
            add(plane, where, value[:, :SIDE] + value[:, SIDE:])

    def step(groups, start, index, _):
        running = []
        for group in range(groups):
            item = start + index * groups + group
            slot = order[jnp.minimum(item, count - 1)]
            weight = jnp.where(item < count, 2.0, 0.0).astype(jnp.float32)
            running.append(stages(place(slot), slot, weight))
        while running:
            running = [machine for machine in running if next(machine, 0) is None]
        return 0

    fours = (count + 1) // 4
    lax.fori_loop(0, fours, functools.partial(step, 4, 0), 0)
    rest = jnp.clip((count - 4 * fours + 1) // 2, 0, 1)
    lax.fori_loop(0, rest, functools.partial(step, 2, 4 * fours), 0)

    def give(block):
        return pltpu.make_async_copy(packed.at[block], grad_hbm.at[block], out_sem.at[block])

    def pack(block, _):
        packed[block] = grad[block].astype(jnp.bfloat16)
        give(block).start()
        return 0

    lax.fori_loop(0, SPAN, pack, 0)
    lax.fori_loop(0, SPAN, lambda block, _: (give(block).wait(), 0)[1], 0)


def grads_call(obj, halo, amp, meta, probe, phase):
    left, right = dft_operands()
    hbm = pl.BlockSpec(memory_space=pl.ANY)
    dma = pltpu.SemaphoreType.DMA
    return pl.pallas_call(
        grads_kernel,
        out_shape=jax.ShapeDtypeStruct((SPAN, 4, 2 * SIDE, SIDE), jnp.bfloat16),
        in_specs=[hbm, hbm, hbm, pl.BlockSpec(memory_space=pltpu.SMEM)] + [hbm] * 4,
        out_specs=hbm,
        scratch_shapes=[
            pltpu.VMEM((4, SPAN, 2 * SIDE, SIDE), jnp.float32),
            pltpu.VMEM((SPAN, 4, 2 * SIDE, SIDE), jnp.float32),
            pltpu.VMEM((4, SIDE, SPAN * SIDE), jnp.float32),
            pltpu.VMEM(halo.shape, halo.dtype),
            pltpu.VMEM(amp.shape, amp.dtype),
            pltpu.VMEM(probe.shape, probe.dtype),
            pltpu.VMEM(phase.shape, phase.dtype),
            pltpu.VMEM(left.shape, jnp.bfloat16),
            pltpu.VMEM(right.shape, jnp.bfloat16),
            pltpu.VMEM((2, SIDE, SIDE), jnp.float32),
            pltpu.VMEM((SPAN, 4, 2 * SIDE, SIDE), jnp.bfloat16),
            pltpu.SMEM((65,), jnp.int32),
            dma((7,)),
            dma((SPAN,)),
        ],
        compiler_params=pltpu.CompilerParams(vmem_limit_bytes=56 * 2**20),
        name="window_gradients",
    )(obj, halo, amp, meta, probe, phase, jnp.asarray(left), jnp.asarray(right))


def send_kernel(obj_ref, measured_ref, offsets_ref, halo_ref, amp_ref, meta_ref,
                wide, extra, measured, chunk, amp_out, meta_out, local_sem, halo_send, halo_recv, amp_send, amp_recv, meta_send, meta_recv, twin_send, twin_recv):
    strip, pos = lax.axis_index("obj"), lax.axis_index("pos")
    x, core = pos // 2, pos % 2
    twin = (strip, x * 2 + 1 - core)

    def span(block):
        return pl.ds(pl.multiple_of(block * SIDE, SIDE), 2 * SIDE)

    loads = [
        pltpu.make_async_copy(obj_ref.at[:, :, span(8 * core + 2 * x)], wide, local_sem.at[0]),
        pltpu.make_async_copy(obj_ref.at[x, :, span(8 - 2 * core)], extra, local_sem.at[1]),
        pltpu.make_async_copy(measured_ref, measured, local_sem.at[2]),
    ]
    for load in loads:
        load.start()
    barrier = pltpu.get_barrier_semaphore()

    def greet_strip(step, _):
        pl.semaphore_signal(barrier, inc=1, device_id=(lax.rem(strip + step, 16), pos), device_id_type=MESH)
        return 0

    lax.fori_loop(1, 16, greet_strip, 0)
    for step in range(1, 4):
        other = lax.rem(x + step, 4) * 2 + core
        pl.semaphore_signal(barrier, inc=1, device_id=(strip, other), device_id_type=MESH)
    pl.semaphore_signal(barrier, inc=1, device_id=twin, device_id_type=MESH)
    loads[0].wait()
    loads[1].wait()
    for block in range(2):
        lanes = slice(block * SIDE, (block + 1) * SIDE)
        for plane in range(4):
            chunk[plane * 2 + block] = wide[plane, :, lanes].astype(jnp.bfloat16)
        chunk[8 + block] = extra[:, lanes].astype(jnp.bfloat16)
    pl.semaphore_wait(barrier, 19)

    def spread(source, index, where, send):
        return pltpu.make_async_remote_copy(
            src_ref=source, dst_ref=halo_ref.at[index], send_sem=halo_send.at[send], recv_sem=halo_recv.at[index],
            device_id=where, device_id_type=MESH,
        )

    first = spread(chunk, x, (lax.rem(strip + 15, 16), pos), 0)
    first.start()

    def amp_copy(target, source):
        return pltpu.make_async_remote_copy(
            src_ref=amp_out.at[target], dst_ref=amp_ref.at[core, source], send_sem=amp_send.at[target],
            recv_sem=amp_recv.at[source], device_id=(target, pos), device_id_type=MESH,
        )

    def meta_copy(target, source):
        return pltpu.make_async_remote_copy(
            src_ref=meta_out.at[target], dst_ref=meta_ref.at[core, source], send_sem=meta_send.at[target],
            recv_sem=meta_recv.at[source], device_id=(target, pos), device_id_type=MESH,
        )

    def to_twin(source, side):
        return pltpu.make_async_remote_copy(
            src_ref=amp_ref.at[core, source], dst_ref=amp_ref.at[side, source], send_sem=twin_send.at[source],
            recv_sem=twin_recv.at[source], device_id=twin, device_id_type=MESH,
        )

    def meta_to_twin(side):
        return pltpu.make_async_remote_copy(
            src_ref=meta_ref.at[core], dst_ref=meta_ref.at[side], send_sem=twin_send.at[16],
            recv_sem=twin_recv.at[16], device_id=twin, device_id_type=MESH,
        )

    lane = lax.broadcasted_iota(jnp.int32, (8, SIDE), 1)
    loads[2].wait()

    def packed(target):
        where, codes, seen = [jnp.int32(0)] * CAP, [jnp.int32(0)] * CAP, jnp.int32(0)
        for item in range(offsets_ref.shape[0]):
            row, col = offsets_ref[item, 0], offsets_ref[item, 1]
            here = row // SIDE == target
            for k in range(CAP):
                take = here & (seen == k)
                where[k] = jnp.where(take, item, where[k])
                codes[k] = jnp.where(take, 1 + row % SIDE * 2048 + col, codes[k])
            seen = seen + here.astype(jnp.int32)
        return jnp.where(lane == 0, codes[0], codes[1]), [coded(measured[index]) for index in where]

    def pack(step, _):
        target = lax.rem(strip + step, 16)
        codes, values = packed(target)
        meta_out[target] = codes
        for k in range(CAP):
            amp_out[target, k] = values[k]
        amp_copy(target, strip).start()
        meta_copy(target, strip).start()
        return 0

    lax.fori_loop(1, 16, pack, 0)
    codes, values = packed(strip)
    meta_ref[core, strip] = codes
    for k in range(CAP):
        amp_ref[core, strip, k] = values[k]
    to_twin(strip, core).start()

    first.wait_recv()
    sends = [first]
    for step in (2, 1, 3):
        copy = spread(halo_ref.at[x], x, (strip, lax.rem(x + step, 4) * 2 + core), step)
        copy.start()
        sends.append(copy)

    def relay(step, _):
        source = lax.rem(strip + 16 - step, 16)
        amp_copy(source, source).wait_recv()
        meta_copy(source, source).wait_recv()
        to_twin(source, core).start()
        return 0

    lax.fori_loop(1, 16, relay, 0)
    meta_to_twin(core).start()

    def finish(step, _):
        target = lax.rem(strip + step, 16)
        amp_copy(target, strip).wait_send()
        meta_copy(target, strip).wait_send()
        return 0

    lax.fori_loop(1, 16, finish, 0)

    def finish_twin(source, _):
        to_twin(source, core).wait_send()
        to_twin(source, 1 - core).wait_recv()
        return 0

    lax.fori_loop(0, 16, finish_twin, 0)
    meta_to_twin(core).wait_send()
    meta_to_twin(1 - core).wait_recv()
    for step in (1, 3, 2):
        spread(chunk, lax.rem(x + step, 4), (strip, pos), 0).wait_recv()
    for copy in sends:
        copy.wait_send()


def send_call(obj, measured, offsets):
    hbm = pl.BlockSpec(memory_space=pl.ANY)
    vmem = pl.BlockSpec(memory_space=pltpu.VMEM)
    dma = pltpu.SemaphoreType.DMA
    return pl.pallas_call(
        send_kernel,
        out_shape=(
            jax.ShapeDtypeStruct((4, 10, SIDE, SIDE), jnp.bfloat16),
            jax.ShapeDtypeStruct((2, 16, CAP, SIDE, SIDE), AMP),
            jax.ShapeDtypeStruct((2, 16, 8, SIDE), jnp.int32),
        ),
        in_specs=[hbm, hbm, pl.BlockSpec(memory_space=pltpu.SMEM)],
        out_specs=(vmem, vmem, vmem),
        scratch_shapes=[
            pltpu.VMEM((4, SIDE, 2 * SIDE), jnp.float32),
            pltpu.VMEM((SIDE, 2 * SIDE), jnp.float32),
            pltpu.VMEM(measured.shape, jnp.float32),
            pltpu.VMEM((10, SIDE, SIDE), jnp.bfloat16),
            pltpu.VMEM((16, CAP, SIDE, SIDE), AMP),
            pltpu.VMEM((16, 8, SIDE), jnp.int32),
            dma((3,)),
            dma((4,)),
            dma((4,)),
            dma((16,)),
            dma((16,)),
            dma((16,)),
            dma((16,)),
            dma((17,)),
            dma((17,)),
        ],
        compiler_params=pltpu.CompilerParams(collective_id=0, has_side_effects=True, vmem_limit_bytes=40 * 2**20),
        name="exchange_inputs",
    )(obj, measured, offsets)


def sum_kernel(grad_ref, out_ref, mine, theirs, joined, parts, low_in, low_out, local_sem, twin_send, twin_recv, x_send, x_recv, low_send, low_recv):
    strip, pos = lax.axis_index("obj"), lax.axis_index("pos")
    x, core = pos // 2, pos % 2
    twin = (strip, x * 2 + 1 - core)
    below, above = (lax.rem(strip + 1, 16), pos), (lax.rem(strip + 15, 16), pos)
    shared = 3 - 3 * core
    load = pltpu.make_async_copy(grad_ref.at[pl.ds(2 * shared + 2 * core, 2)], mine, local_sem)
    load.start()
    barrier = pltpu.get_barrier_semaphore()
    for step in range(1, 8):
        pl.semaphore_signal(barrier, inc=1, device_id=(strip, lax.rem(pos + step, 8)), device_id_type=MESH)
    for device in (below, above):
        pl.semaphore_signal(barrier, inc=1, device_id=device, device_id_type=MESH)
    pl.semaphore_wait(barrier, 9)
    to_twin = pltpu.make_async_remote_copy(
        src_ref=grad_ref.at[pl.ds(8 - 8 * core, 2)], dst_ref=theirs, send_sem=twin_send, recv_sem=twin_recv,
        device_id=twin, device_id_type=MESH,
    )
    to_twin.start()
    halves = (pl.ds(SIDE, SIDE), pl.ds(0, SIDE))

    def remote(pair, source, half, target, start):
        return pltpu.make_async_remote_copy(
            src_ref=source.at[:, :, halves[half]], dst_ref=parts.at[start, half], send_sem=x_send.at[pair, half],
            recv_sem=x_recv.at[start, half], device_id=(strip, target), device_id_type=MESH,
        )

    def local(source, half):
        return pltpu.make_async_copy(source.at[:, :, halves[half]], parts.at[x, half], x_recv.at[x, half])

    def give(pair, source, half):
        target = 4 * core + pair

        @pl.when(target != pos)
        def _():
            remote(pair, source, half, target, x).start()

        @pl.when(target == pos)
        def _():
            local(source, half).start()

    def block_pair(pair):
        return grad_ref.at[pl.ds(2 * pair + 2 * core, 2)]

    pairs = [lax.rem(shared + step, 4) for step in range(1, 4)]
    for half in range(2):
        for pair in pairs:
            give(pair, block_pair(pair), half)
    load.wait()
    to_twin.wait_recv()
    for half in range(2):
        for block in range(2):
            for plane in range(4):
                rows = slice(SIDE, None) if half == 0 else slice(0, SIDE)
                joined[block, plane, rows] = (
                    mine[block, plane, rows].astype(jnp.float32) + theirs[block, plane, rows].astype(jnp.float32)
                ).astype(jnp.bfloat16)
        give(shared, joined, half)

    def arrived(half):
        for start in range(4):
            remote(0, joined, half, pos, start).wait_recv()

    def total(half, block, plane):
        value = parts[0, half, block, plane].astype(jnp.float32)
        for start in range(1, 4):
            value += parts[start, half, block, plane].astype(jnp.float32)
        return value

    arrived(0)
    for block in range(2):
        for plane in range(4):
            low_out[block, plane] = total(0, block, plane).astype(jnp.bfloat16)
    shift = pltpu.make_async_remote_copy(
        src_ref=low_out, dst_ref=low_in, send_sem=low_send, recv_sem=low_recv, device_id=below, device_id_type=MESH,
    )
    shift.start()
    arrived(1)
    shift.wait_recv()
    for block in range(2):
        for plane in range(4):
            out_ref[plane, :, block * SIDE : (block + 1) * SIDE] = total(1, block, plane) + low_in[block, plane].astype(jnp.float32)
    shift.wait_send()
    to_twin.wait_send()
    for half in range(2):
        for pair in range(4):
            target = 4 * core + pair

            @pl.when(target != pos)
            def _():
                remote(pair, joined, half, target, x).wait_send()


def sum_call(grad):
    dma = pltpu.SemaphoreType.DMA
    two = (2, 4, 2 * SIDE, SIDE)
    return pl.pallas_call(
        sum_kernel,
        out_shape=jax.ShapeDtypeStruct((4, SIDE, 2 * SIDE), jnp.float32),
        in_specs=[pl.BlockSpec(memory_space=pl.ANY)],
        out_specs=pl.BlockSpec(memory_space=pltpu.VMEM),
        scratch_shapes=[
            pltpu.VMEM(two, jnp.bfloat16),
            pltpu.VMEM(two, jnp.bfloat16),
            pltpu.VMEM(two, jnp.bfloat16),
            pltpu.VMEM((4, 2, 2, 4, SIDE, SIDE), jnp.bfloat16),
            pltpu.VMEM((2, 4, SIDE, SIDE), jnp.bfloat16),
            pltpu.VMEM((2, 4, SIDE, SIDE), jnp.bfloat16),
            dma,
            dma,
            dma,
            dma((4, 2)),
            dma((4, 2)),
            dma,
            dma,
        ],
        compiler_params=pltpu.CompilerParams(collective_id=1, has_side_effects=True, vmem_limit_bytes=40 * 2**20),
        name="sum_gradients",
    )(grad)


def per_device(object_field, probe_modes, propagator_phase, offsets, measured):
    obj = object_field.reshape(4, SIDE, object_field.shape[3])
    halo, amp, meta = send_call(obj, measured, offsets)
    grad = grads_call(obj, halo, amp, meta, probe_modes, propagator_phase)
    return sum_call(grad).reshape(2, 2, SIDE, 2 * SIDE)


def solution(mesh):
    placed = (
        P(None, None, "obj", None),
        P(),
        P(),
        P(("obj", "pos"), None),
        P(("obj", "pos"), None, None),
    )
    return jax.shard_map(
        per_device,
        mesh=mesh,
        in_specs=placed,
        out_specs=P(None, None, "obj", "pos"),
        check_vma=False,
    )
```

time: 194 us -> 121 us (0.62)
  the two profiles are of different devices: /device:TPU:6 before, /device:TPU:65 now
where the time goes in v2:
time: 121 us; the launch traced here: 120 us
  Pallas kernels  110 us (91%)
  local copies, waits for them, and re-layouts  9.78 us (8%)
    pallas_call x1, Pallas kernels, grads_call(): pl.pallas_call(grads_kernel, out_shape=jax.ShapeDtypeStruct((SPAN, 4, 2 *...  43 us
    pallas_call x1, Pallas kernels, send_call(): pl.pallas_call(send_kernel, out_shape=(jax.ShapeDtypeStruct((4, 10, SIDE,...  39.6 us
    pallas_call x1, Pallas kernels, sum_call(): pl.pallas_call(sum_kernel, out_shape=jax.ShapeDtypeStruct((4, SIDE, 2 * S...  27.8 us
    unnamed x14, local copies, waits for them, and re-layouts  9.78 us

profile of v2, /device:TPU:65, one launch (start us, length us, event | category | flops | bytes accessed | tf_op | source)
XLA Modules:
  0.0 120.3 jit_solution(15732374414637666153)
XLA Ops:
  0.0 0.8 copy.8.offsets_ref
  0.8 0.0 copy-start
  0.8 2.2 %copy-done = f32[2,2,128,2048]{3,2,1,0:T(8,128)S(1)} copy-done((f32[2,2,128,2048]{3,2,1,0:T(8,128)S(1)}, f32[2,2,128,2048]{3,2,1,0:T(8,128)}, u32[]{:S(2)}) %copy-start) | copy-done | bytes 4194328
  2.9 0.0 copy-start.4
  2.9 1.2 %copy-done.4 = f32[16,128,128]{2,1,0:T(8,128)S(1)} copy-done((f32[16,128,128]{2,1,0:T(8,128)S(1)}, f32[16,128,128]{2,1,0:T(8,128)}, u32[]{:S(2)}) %copy-start.4) | copy-done | bytes 1048600
  4.2 39.6 %exchange_inputs.1 = (bf16[4,10,128,128]{3,2,1,0:T(8,128)(2,1)S(1)}, s16[2,16,2,128,128]{4,3,2,1,0:T(8,128)(2,1)S(1)}, s32[2,16,8,128]{3,2,1,0:T(8,128)S(1)}) custom-call(f32[4,128,2048]{2,1,0:T(8,128)S(1)} %bitcast.3, f32[16,128,128]{2,1,0:T(8,128)S(1)} %copy-done.4, s32[16,2]{1,0:T(8,128)S(1)} %copy.8.offsets_ref), custom_call_target="tpu_custom_call" | custom-call | tf_op jit(solution)/shard_map/exchange_inputs/pallas_call | solution.py:388
  43.8 0.0 copy-start.2
  43.8 1.3 %copy-done.2 = s16[2,16,2,128,128]{4,3,2,1,0:T(8,128)(2,1)} copy-done((s16[2,16,2,128,128]{4,3,2,1,0:T(8,128)(2,1)}, s16[2,16,2,128,128]{4,3,2,1,0:T(8,128)(2,1)S(1)}, u32[]{:S(2)}) %copy-start.2) | copy-done | bytes 2097176
  45.1 0.0 copy-start.3
  45.1 1.1 copy-done.3
  46.3 0.0 copy-start.5
  46.3 0.7 copy-done.5
  46.9 43.0 %window_gradients.1.grad_ref = bf16[10,4,256,128]{3,2,1,0:T(8,128)(2,1)} custom-call(f32[4,128,2048]{2,1,0:T(8,128)} %bitcast.2, bf16[4,10,128,128]{3,2,1,0:T(8,128)(2,1)} %copy-done.3, s16[2,16,2,128,128]{4,3,2,1,0:T(8,128)(2,1)} %copy-done.2, s32[2,16,8,128]{3,2,1,0:T(8,128)} %copy-done.5, f32[2,2,128,128]{3,2,1,0:T(8,128)} %probe_hbm.1, ...), custom_call_target="tpu_custom_call" | custom-call | tf_op jit(solution)/shard_map/window_gradients/pallas_call | solution.py:218
  89.9 0.0 copy-start.1
  89.9 1.7 %copy-done.1 = bf16[10,4,256,128]{3,2,1,0:T(8,128)(2,1)S(1)} copy-done((bf16[10,4,256,128]{3,2,1,0:T(8,128)(2,1)S(1)}, bf16[10,4,256,128]{3,2,1,0:T(8,128)(2,1)}, u32[]{:S(2)}) %copy-start.1) | copy-done | bytes 2621464
  91.6 27.8 %sum_gradients.1 = f32[4,128,256]{2,1,0:T(8,128)S(1)} custom-call(bf16[10,4,256,128]{3,2,1,0:T(8,128)(2,1)S(1)} %copy-done.1), custom_call_target="tpu_custom_call" | custom-call | tf_op jit(solution)/shard_map/sum_gradients/pallas_call | solution.py:515
  119.5 0.8 copy.10
Async XLA Ops:
  0.8 2.2 %copy-start = (f32[2,2,128,2048]{3,2,1,0:T(8,128)S(1)}, f32[2,2,128,2048]{3,2,1,0:T(8,128)}, u32[]{:S(2)}) copy-start(f32[2,2,128,2048]{3,2,1,0:T(8,128)} %param.7) | copy-start | bytes 12582916
  2.9 1.2 %copy-start.4 = (f32[16,128,128]{2,1,0:T(8,128)S(1)}, f32[16,128,128]{2,1,0:T(8,128)}, u32[]{:S(2)}) copy-start(f32[16,128,128]{2,1,0:T(8,128)} %measured_ref.1) | copy-start | bytes 3145732
  43.8 1.3 %copy-start.2 = (s16[2,16,2,128,128]{4,3,2,1,0:T(8,128)(2,1)}, s16[2,16,2,128,128]{4,3,2,1,0:T(8,128)(2,1)S(1)}, u32[]{:S(2)}) copy-start(s16[2,16,2,128,128]{4,3,2,1,0:T(8,128)(2,1)S(1)} %get-tuple-element.9.amp_hbm) | copy-start | bytes 6291460
  45.1 1.1 copy-start.3
  46.3 0.7 copy-start.5
  89.9 1.7 %copy-start.1 = (bf16[10,4,256,128]{3,2,1,0:T(8,128)(2,1)S(1)}, bf16[10,4,256,128]{3,2,1,0:T(8,128)(2,1)}, u32[]{:S(2)}) copy-start(bf16[10,4,256,128]{3,2,1,0:T(8,128)(2,1)} %window_gradients.1.grad_ref) | copy-start | bytes 7864324

commit v3 on v2

--- a/solution.py
+++ b/solution.py
@@ -11,6 +11,9 @@
 
 CAP = 2
 SIDE = 128
+META_TILE = (1, 128)
+PIECES = 5
+K2_LIMIT = 30
 SPAN = 10
 LOW_COL, HIGH_COL = 768, 1152
 AMP = jnp.int16
@@ -67,25 +70,36 @@
     return out_real, out_imag
 
 
-def grads_kernel(obj_ref, halo_ref, amp_hbm, meta_ref, probe_hbm, phase_hbm, left_hbm, right_hbm, grad_hbm,
-                 field, grad, own, halo, amp, probe, phase, left_ref, right_ref, prop_ref, packed, order, sems, out_sem):
+def grads_kernel(obj_ref, halo, amp, meta_hbm, probe, phase, left_hbm, right_hbm, packed,
+                 field, grad, prop_ref, left_ref, right_ref, meta_ref, order, sems):
     core = lax.axis_index("pos") % 2
     base = 6 * core
-    columns = pl.ds(pl.multiple_of(base * SIDE, SIDE), SPAN * SIDE)
-    loads = [
-        pltpu.make_async_copy(source, target, sems.at[k])
-        for k, (source, target) in enumerate([
-            (obj_ref.at[:, :, columns], own),
-            (halo_ref, halo),
-            (phase_hbm, phase),
-            (probe_hbm, probe),
-            (left_hbm, left_ref),
-            (right_hbm, right_ref),
-            (amp_hbm, amp),
-        ])
-    ]
-    for load in loads:
-        load.start()
+    meta_load = pltpu.make_async_copy(meta_hbm, meta_ref, sems.at[0])
+    meta_load.start()
+    left_load = pltpu.make_async_copy(left_hbm, left_ref, sems.at[1])
+    left_load.start()
+    right_load = pltpu.make_async_copy(right_hbm, right_ref, sems.at[2])
+    right_load.start()
+
+    def widen(index, _):
+        plane, block = index // SPAN, index % SPAN
+        inside = block + base - 8 * core
+        within = (inside >= 0) & (inside < 8)
+        extra = block + base - (8 - 2 * core)
+        part = jnp.where(within, inside // 2, plane)
+        tile = jnp.where(within, plane * 2 + inside % 2, 8 + extra)
+        span = pl.ds(pl.multiple_of((base + block) * SIDE, SIDE), SIDE)
+        field[plane, block, :SIDE, :] = obj_ref[plane, :, span].astype(jnp.bfloat16).astype(jnp.float32)
+        field[plane, block, SIDE:, :] = halo[part, tile].astype(jnp.float32)
+        grad[block, plane] = jnp.zeros((2 * SIDE, SIDE), jnp.float32)
+        return 0
+
+    lax.fori_loop(0, 4 * SPAN, widen, 0)
+    prop_ref[0] = jnp.cos(phase[...])
+    prop_ref[1] = jnp.sin(phase[...])
+    meta_load.wait()
+    left_load.wait()
+    right_load.wait()
 
     def read(slot):
         code = meta_ref[slot // 32, slot % 32 // 2, 0, slot % 2] - 1
@@ -98,7 +112,7 @@
         last = here * (col > HIGH_COL).astype(jnp.int32)
         return counts[0] + here, counts[1] + first, counts[2] + last
 
-    whole, first_only, last_only = lax.fori_loop(0, 64, tally, (0, 0, 0))
+    whole, first_only, last_only = lax.fori_loop(0, 64, tally, (0, 0, 0), unroll=8)
     either = whole - first_only - last_only
     to_first = jnp.clip((whole + 1) // 2 - first_only, 0, either)
 
@@ -111,29 +125,7 @@
         mine = valid & (on_first == (core == 0))
         return count + mine.astype(jnp.int32), seen + (valid & free).astype(jnp.int32)
 
-    count, _ = lax.fori_loop(0, 64, collect, (0, 0))
-    loads[0].wait()
-    loads[1].wait()
-
-    def widen(index, _):
-        plane, block = index // SPAN, index % SPAN
-        inside = block + base - 8 * core
-        within = (inside >= 0) & (inside < 8)
-        extra = block + base - (8 - 2 * core)
-        part = jnp.where(within, inside // 2, plane)
-        tile = jnp.where(within, plane * 2 + inside % 2, 8 + extra)
-        span = pl.ds(pl.multiple_of(block * SIDE, SIDE), SIDE)
-        field[plane, block, :SIDE, :] = own[plane, :, span].astype(jnp.bfloat16).astype(jnp.float32)
-        field[plane, block, SIDE:, :] = halo[part, tile].astype(jnp.float32)
-        grad[block, plane] = jnp.zeros((2 * SIDE, SIDE), jnp.float32)
-        return 0
-
-    lax.fori_loop(0, 4 * SPAN, widen, 0)
-    loads[2].wait()
-    prop_ref[0] = jnp.cos(phase[...])
-    prop_ref[1] = jnp.sin(phase[...])
-    for load in loads[3:]:
-        load.wait()
+    count, _ = lax.fori_loop(0, 64, collect, (0, 0), unroll=8)
     lane = lax.broadcasted_iota(jnp.int32, (SIDE, SIDE), 1)
 
     def place(slot):
@@ -199,46 +191,35 @@
     rest = jnp.clip((count - 4 * fours + 1) // 2, 0, 1)
     lax.fori_loop(0, rest, functools.partial(step, 2, 4 * fours), 0)
 
-    def give(block):
-        return pltpu.make_async_copy(packed.at[block], grad_hbm.at[block], out_sem.at[block])
-
     def pack(block, _):
         packed[block] = grad[block].astype(jnp.bfloat16)
-        give(block).start()
         return 0
 
     lax.fori_loop(0, SPAN, pack, 0)
-    lax.fori_loop(0, SPAN, lambda block, _: (give(block).wait(), 0)[1], 0)
 
 
 def grads_call(obj, halo, amp, meta, probe, phase):
-    left, right = dft_operands()
-    hbm = pl.BlockSpec(memory_space=pl.ANY)
-    dma = pltpu.SemaphoreType.DMA
+    left, right = [pltpu.with_memory_space_constraint(jnp.asarray(x), pltpu.HBM) for x in dft_operands()]
+    hbm = pl.BlockSpec(memory_space=pltpu.HBM)
+    vmem = pl.BlockSpec(memory_space=pltpu.VMEM)
     return pl.pallas_call(
         grads_kernel,
         out_shape=jax.ShapeDtypeStruct((SPAN, 4, 2 * SIDE, SIDE), jnp.bfloat16),
-        in_specs=[hbm, hbm, hbm, pl.BlockSpec(memory_space=pltpu.SMEM)] + [hbm] * 4,
-        out_specs=hbm,
+        in_specs=[vmem] * 6 + [hbm] * 2,
+        out_specs=vmem,
         scratch_shapes=[
             pltpu.VMEM((4, SPAN, 2 * SIDE, SIDE), jnp.float32),
             pltpu.VMEM((SPAN, 4, 2 * SIDE, SIDE), jnp.float32),
-            pltpu.VMEM((4, SIDE, SPAN * SIDE), jnp.float32),
-            pltpu.VMEM(halo.shape, halo.dtype),
-            pltpu.VMEM(amp.shape, amp.dtype),
-            pltpu.VMEM(probe.shape, probe.dtype),
-            pltpu.VMEM(phase.shape, phase.dtype),
+            pltpu.VMEM((2, SIDE, SIDE), jnp.float32),
             pltpu.VMEM(left.shape, jnp.bfloat16),
             pltpu.VMEM(right.shape, jnp.bfloat16),
-            pltpu.VMEM((2, SIDE, SIDE), jnp.float32),
-            pltpu.VMEM((SPAN, 4, 2 * SIDE, SIDE), jnp.bfloat16),
+            pltpu.SMEM(meta.shape, jnp.int32),
             pltpu.SMEM((65,), jnp.int32),
-            dma((7,)),
-            dma((SPAN,)),
+            pltpu.SemaphoreType.DMA((3,)),
         ],
-        compiler_params=pltpu.CompilerParams(vmem_limit_bytes=56 * 2**20),
+        compiler_params=pltpu.CompilerParams(vmem_limit_bytes=K2_LIMIT * 2**20),
         name="window_gradients",
-    )(obj, halo, amp, meta, probe, phase, jnp.asarray(left), jnp.asarray(right))
+    )(obj, halo, amp, meta, probe, phase, left, right)
 
 
 def send_kernel(obj_ref, measured_ref, offsets_ref, halo_ref, amp_ref, meta_ref,
@@ -277,14 +258,18 @@
         chunk[8 + block] = extra[:, lanes].astype(jnp.bfloat16)
     pl.semaphore_wait(barrier, 19)
 
-    def spread(source, index, where, send):
+    def piece(number):
+        return pl.ds(number * (10 // PIECES), 10 // PIECES)
+
+    def spread(source, index, number, where, send):
         return pltpu.make_async_remote_copy(
-            src_ref=source, dst_ref=halo_ref.at[index], send_sem=halo_send.at[send], recv_sem=halo_recv.at[index],
-            device_id=where, device_id_type=MESH,
+            src_ref=source.at[piece(number)], dst_ref=halo_ref.at[index, piece(number)], send_sem=halo_send.at[send, number],
+            recv_sem=halo_recv.at[index, number], device_id=where, device_id_type=MESH,
         )
 
-    first = spread(chunk, x, (lax.rem(strip + 15, 16), pos), 0)
-    first.start()
+    above = (lax.rem(strip + 15, 16), pos)
+    for number in range(PIECES):
+        spread(chunk, x, number, above, 0).start()
 
     def amp_copy(target, source):
         return pltpu.make_async_remote_copy(
@@ -310,13 +295,13 @@
             recv_sem=twin_recv.at[16], device_id=twin, device_id_type=MESH,
         )
 
-    lane = lax.broadcasted_iota(jnp.int32, (8, SIDE), 1)
+    lane = lax.broadcasted_iota(jnp.int32, META_TILE, 1)
     loads[2].wait()
 
     def packed(target):
         where, codes, seen = [jnp.int32(0)] * CAP, [jnp.int32(0)] * CAP, jnp.int32(0)
-        for item in range(offsets_ref.shape[0]):
-            row, col = offsets_ref[item, 0], offsets_ref[item, 1]
+        for item in range(offsets_ref.shape[1]):
+            row, col = offsets_ref[0, item], offsets_ref[1, item]
             here = row // SIDE == target
             for k in range(CAP):
                 take = here & (seen == k)
@@ -335,20 +320,22 @@
         meta_copy(target, strip).start()
         return 0
 
-    lax.fori_loop(1, 16, pack, 0)
+    def forward(number):
+        spread(chunk, x, number, above, 0).wait_recv()
+        for step in (2, 1, 3):
+            spread(halo_ref.at[x], x, number, (strip, lax.rem(x + step, 4) * 2 + core), step).start()
+
+    bounds = [1, 6] + [6 + (10 * k) // PIECES for k in range(1, PIECES)] + [16]
+    lax.fori_loop(bounds[0], bounds[1], pack, 0)
+    for number in range(PIECES):
+        forward(number)
+        lax.fori_loop(bounds[number + 1], bounds[number + 2], pack, 0)
     codes, values = packed(strip)
     meta_ref[core, strip] = codes
     for k in range(CAP):
         amp_ref[core, strip, k] = values[k]
     to_twin(strip, core).start()
 
-    first.wait_recv()
-    sends = [first]
-    for step in (2, 1, 3):
-        copy = spread(halo_ref.at[x], x, (strip, lax.rem(x + step, 4) * 2 + core), step)
-        copy.start()
-        sends.append(copy)
-
     def relay(step, _):
         source = lax.rem(strip + 16 - step, 16)
         amp_copy(source, source).wait_recv()
@@ -375,14 +362,15 @@
     lax.fori_loop(0, 16, finish_twin, 0)
     meta_to_twin(core).wait_send()
     meta_to_twin(1 - core).wait_recv()
-    for step in (1, 3, 2):
-        spread(chunk, lax.rem(x + step, 4), (strip, pos), 0).wait_recv()
-    for copy in sends:
-        copy.wait_send()
+    for number in range(PIECES):
+        for step in range(1, 4):
+            spread(chunk, lax.rem(x + step, 4), number, (strip, pos), 0).wait_recv()
+        for step in range(4):
+            spread(chunk, x, number, (strip, pos), step).wait_send()
 
 
 def send_call(obj, measured, offsets):
-    hbm = pl.BlockSpec(memory_space=pl.ANY)
+    hbm = pl.BlockSpec(memory_space=pltpu.HBM)
     vmem = pl.BlockSpec(memory_space=pltpu.VMEM)
     dma = pltpu.SemaphoreType.DMA
     return pl.pallas_call(
@@ -390,7 +378,7 @@
         out_shape=(
             jax.ShapeDtypeStruct((4, 10, SIDE, SIDE), jnp.bfloat16),
             jax.ShapeDtypeStruct((2, 16, CAP, SIDE, SIDE), AMP),
-            jax.ShapeDtypeStruct((2, 16, 8, SIDE), jnp.int32),
+            jax.ShapeDtypeStruct((2, 16, *META_TILE), jnp.int32),
         ),
         in_specs=[hbm, hbm, pl.BlockSpec(memory_space=pltpu.SMEM)],
         out_specs=(vmem, vmem, vmem),
@@ -400,10 +388,10 @@
             pltpu.VMEM(measured.shape, jnp.float32),
             pltpu.VMEM((10, SIDE, SIDE), jnp.bfloat16),
             pltpu.VMEM((16, CAP, SIDE, SIDE), AMP),
-            pltpu.VMEM((16, 8, SIDE), jnp.int32),
+            pltpu.VMEM((16, *META_TILE), jnp.int32),
             dma((3,)),
-            dma((4,)),
-            dma((4,)),
+            dma((4, PIECES)),
+            dma((4, PIECES)),
             dma((16,)),
             dma((16,)),
             dma((16,)),
@@ -411,19 +399,20 @@
             dma((17,)),
             dma((17,)),
         ],
-        compiler_params=pltpu.CompilerParams(collective_id=0, has_side_effects=True, vmem_limit_bytes=40 * 2**20),
+        compiler_params=pltpu.CompilerParams(collective_id=0, has_side_effects=True, vmem_limit_bytes=16 * 2**20),
         name="exchange_inputs",
-    )(obj, measured, offsets)
-
-
-def sum_kernel(grad_ref, out_ref, mine, theirs, joined, parts, low_in, low_out, local_sem, twin_send, twin_recv, x_send, x_recv, low_send, low_recv):
+    )(
+        pltpu.with_memory_space_constraint(obj, pltpu.HBM), pltpu.with_memory_space_constraint(measured, pltpu.HBM), offsets
+    )
+
+
+def sum_kernel(grad_ref, out_ref, theirs, joined, parts, low_in, low_out, twin_send, twin_recv, x_send, x_recv, low_send, low_recv):
     strip, pos = lax.axis_index("obj"), lax.axis_index("pos")
     x, core = pos // 2, pos % 2
     twin = (strip, x * 2 + 1 - core)
     below, above = (lax.rem(strip + 1, 16), pos), (lax.rem(strip + 15, 16), pos)
     shared = 3 - 3 * core
-    load = pltpu.make_async_copy(grad_ref.at[pl.ds(2 * shared + 2 * core, 2)], mine, local_sem)
-    load.start()
+    mine = 2 * shared + 2 * core
     barrier = pltpu.get_barrier_semaphore()
     for step in range(1, 8):
         pl.semaphore_signal(barrier, inc=1, device_id=(strip, lax.rem(pos + step, 8)), device_id_type=MESH)
@@ -464,14 +453,13 @@
     for half in range(2):
         for pair in pairs:
             give(pair, block_pair(pair), half)
-    load.wait()
     to_twin.wait_recv()
     for half in range(2):
         for block in range(2):
             for plane in range(4):
                 rows = slice(SIDE, None) if half == 0 else slice(0, SIDE)
                 joined[block, plane, rows] = (
-                    mine[block, plane, rows].astype(jnp.float32) + theirs[block, plane, rows].astype(jnp.float32)
+                    grad_ref[mine + block, plane, rows].astype(jnp.float32) + theirs[block, plane, rows].astype(jnp.float32)
                 ).astype(jnp.bfloat16)
         give(shared, joined, half)
 
@@ -515,10 +503,9 @@
     return pl.pallas_call(
         sum_kernel,
         out_shape=jax.ShapeDtypeStruct((4, SIDE, 2 * SIDE), jnp.float32),
-        in_specs=[pl.BlockSpec(memory_space=pl.ANY)],
+        in_specs=[pl.BlockSpec(memory_space=pltpu.VMEM)],
         out_specs=pl.BlockSpec(memory_space=pltpu.VMEM),
         scratch_shapes=[
-            pltpu.VMEM(two, jnp.bfloat16),
             pltpu.VMEM(two, jnp.bfloat16),
             pltpu.VMEM(two, jnp.bfloat16),
             pltpu.VMEM((4, 2, 2, 4, SIDE, SIDE), jnp.bfloat16),
@@ -526,20 +513,19 @@
             pltpu.VMEM((2, 4, SIDE, SIDE), jnp.bfloat16),
             dma,
             dma,
-            dma,
             dma((4, 2)),
             dma((4, 2)),
             dma,
             dma,
         ],
-        compiler_params=pltpu.CompilerParams(collective_id=1, has_side_effects=True, vmem_limit_bytes=40 * 2**20),
+        compiler_params=pltpu.CompilerParams(collective_id=1, has_side_effects=True, vmem_limit_bytes=20 * 2**20),
         name="sum_gradients",
     )(grad)
 
 
 def per_device(object_field, probe_modes, propagator_phase, offsets, measured):
     obj = object_field.reshape(4, SIDE, object_field.shape[3])
-    halo, amp, meta = send_call(obj, measured, offsets)
+    halo, amp, meta = send_call(obj, measured, offsets.T)
     grad = grads_call(obj, halo, amp, meta, probe_modes, propagator_phase)
     return sum_call(grad).reshape(2, 2, SIDE, 2 * SIDE)
 

time: 121 us -> 96.9 us (0.80)
  the two profiles are of different devices: /device:TPU:65 before, /device:TPU:1 now
where the time goes in v3:
time: 96.9 us; the launch traced here: 96.3 us
  Pallas kernels  94.7 us (98%)
  local copies, waits for them, and re-layouts  1.49 us (2%)
    pallas_call x1, Pallas kernels, sum_call(): pl.pallas_call(sum_kernel, out_shape=jax.ShapeDtypeStruct((4, SIDE, 2 * S...  33.6 us
    pallas_call x1, Pallas kernels, send_call(): pl.pallas_call(send_kernel, out_shape=(jax.ShapeDtypeStruct((4, 10, SIDE,...  33.2 us
    pallas_call x1, Pallas kernels, grads_call(): pl.pallas_call(grads_kernel, out_shape=jax.ShapeDtypeStruct((SPAN, 4, 2 *...  27.9 us

profile of v3, /device:TPU:1, one launch (start us, length us, event | category | flops | bytes accessed | tf_op | source)
XLA Modules:
  0.0 96.3 jit_solution(11241836149243199179)
XLA Ops:
  0.0 0.0 copy-start.3
  0.0 0.7 copy-done.3
  0.7 0.0 copy-start
  0.7 0.0 copy-start.1
  0.7 0.0 copy-start.2
  0.7 33.2 %exchange_inputs.1 = (bf16[4,10,128,128]{3,2,1,0:T(8,128)(2,1)S(1)}, s16[2,16,2,128,128]{4,3,2,1,0:T(8,128)(2,1)S(1)}, s32[2,16,1,128]{3,2,1,0:T(1,128)S(1)}) custom-call(f32[4,128,2048]{2,1,0:T(8,128)} %bitcast.3, f32[16,128,128]{2,1,0:T(8,128)} %measured_ref.1, s32[2,16]{1,0:T(2,128)S(1)} %bitcast.6), custom_call_target="tpu_custom_call" | custom-call | tf_op jit(solution)/shard_map/exchange_inputs/pallas_call | solution.py:376
  33.9 0.0 copy-done
  33.9 0.0 copy-done.1
  33.9 0.0 copy-done.2
  33.9 27.9 %window_gradients.1.grad_ref = bf16[10,4,256,128]{3,2,1,0:T(8,128)(2,1)S(1)} custom-call(f32[4,128,2048]{2,1,0:T(8,128)S(1)} %bitcast.4, bf16[4,10,128,128]{3,2,1,0:T(8,128)(2,1)S(1)} %get-tuple-element.8.halo, s16[2,16,2,128,128]{4,3,2,1,0:T(8,128)(2,1)S(1)} %get-tuple-element.9.amp, s32[2,16,1,128]{3,2,1,0:T(1,128)S(1)} %get-tuple-element.10.meta_hbm, ...), custom_call_target="tpu_custom_call" | custom-call | tf_op jit(solution)/shard_map/window_gradients/pallas_call | solution.py:205
  61.9 33.6 %sum_gradients.1 = f32[4,128,256]{2,1,0:T(8,128)S(1)} custom-call(bf16[10,4,256,128]{3,2,1,0:T(8,128)(2,1)S(1)} %window_gradients.1.grad_ref), custom_call_target="tpu_custom_call" | custom-call | tf_op jit(solution)/shard_map/sum_gradients/pallas_call | solution.py:503
  95.5 0.8 copy.9
Async XLA Ops:
  0.0 0.7 copy-start.3
  0.7 33.2 %copy-start = (f32[2,2,128,2048]{3,2,1,0:T(8,128)S(1)}, f32[2,2,128,2048]{3,2,1,0:T(8,128)}, u32[]{:S(2)}) copy-start(f32[2,2,128,2048]{3,2,1,0:T(8,128)} %param.7) | copy-start | bytes 12582916
  0.7 33.2 %copy-start.1 = (f32[2,2,128,128]{3,2,1,0:T(8,128)S(1)}, f32[2,2,128,128]{3,2,1,0:T(8,128)}, u32[]{:S(2)}) copy-start(f32[2,2,128,128]{3,2,1,0:T(8,128)} %probe.1) | copy-start | bytes 786436
  0.7 33.3 %copy-start.2 = (f32[128,128]{1,0:T(8,128)S(1)}, f32[128,128]{1,0:T(8,128)}, u32[]{:S(2)}) copy-start(f32[128,128]{1,0:T(8,128)} %phase.1) | copy-start | bytes 196612

commit v4 on v3

--- a/solution.py
+++ b/solution.py
@@ -24,82 +24,105 @@
 def dft_operands():
     index = np.arange(SIDE)
     angles = (index[:, None] * index[None, :] % SIDE) * (2.0 * math.pi / SIDE)
-    cosine = np.cos(angles) / math.sqrt(SIDE)
-    sine = np.sin(angles) / math.sqrt(SIDE)
-
-    def parts(block, axis):
+    wave = np.cos(angles) / math.sqrt(SIDE)
+    wave[SIDE // 2 + 1 :] = np.sin(angles[1 : SIDE // 2]) / math.sqrt(SIDE)
+
+    def product(block):
         block = block.astype(np.float32)
         high = block.astype(jnp.bfloat16)
         low = (block - high.astype(np.float32)).astype(jnp.bfloat16)
-        return np.concatenate([high, low, high], axis=axis)
-
-    left, right = [], []
-    for sign in (1.0, -1.0):
-        s = sign * sine
-        left.append(parts(np.block([[cosine, s], [-s, cosine]]), 1))
-        right.append(parts(np.block([[cosine, -s], [s, cosine]]), 0))
-    return np.stack(left), np.stack(right)
+        return np.block([[high, high], [low, np.zeros_like(low)]])
+
+    order = np.zeros((SIDE, SIDE), jnp.bfloat16)
+    order[index, np.where(index <= SIDE // 2, index, SIDE + SIDE // 2 - index)] = 1
+    return np.stack([product(wave), product(wave.T)]), order
 
 
 def coded(measured):
-    return jnp.round((jnp.sqrt(measured) - AMP_MIDDLE) * AMP_STEPS).astype(jnp.int32).astype(AMP)
+    return jnp.round((jnp.sqrt(measured) - AMP_MIDDLE) * AMP_STEPS)
 
 
 def decoded(code):
     return code.astype(jnp.int32).astype(jnp.float32) * (1.0 / AMP_STEPS) + AMP_MIDDLE
 
 
-def split3(x, axis):
+def multiply(left, planes):
+    x = jnp.concatenate(planes, axis=1)
     high = x.astype(jnp.bfloat16)
     low = (x - high.astype(jnp.float32)).astype(jnp.bfloat16)
-    return jnp.concatenate([high, high, low], axis=axis)
-
-
-def transform2d(left, right, which, real, imag):
-    fields = real.shape[1] // SIDE
-    y = jnp.dot(left[which], split3(jnp.concatenate([real, imag], axis=0), 0), preferred_element_type=jnp.float32)
-    yield
-    rows = [
-        jnp.concatenate([y[:SIDE, k * SIDE : (k + 1) * SIDE], y[SIDE:, k * SIDE : (k + 1) * SIDE]], axis=1)
-        for k in range(fields)
-    ]
-    z = jnp.dot(split3(jnp.concatenate(rows, axis=0), 1), right[which], preferred_element_type=jnp.float32)
-    yield
-    out_real = jnp.concatenate([z[k * SIDE : (k + 1) * SIDE, :SIDE] for k in range(fields)], axis=1)
-    out_imag = jnp.concatenate([z[k * SIDE : (k + 1) * SIDE, SIDE:] for k in range(fields)], axis=1)
-    return out_real, out_imag
-
-
-def grads_kernel(obj_ref, halo, amp, meta_hbm, probe, phase, left_hbm, right_hbm, packed,
-                 field, grad, prop_ref, left_ref, right_ref, meta_ref, order, sems):
+    y = jnp.dot(left, jnp.concatenate([high, low], axis=0), preferred_element_type=jnp.float32)
+    y = y[:SIDE] + y[SIDE:]
+    return [y[:, k * SIDE : (k + 1) * SIDE] for k in range(len(planes))]
+
+
+def halves(plane):
+    return plane[: SIDE // 2], plane[SIDE // 2 :]
+
+
+def with_first_row(first, rest):
+    row = lax.broadcasted_iota(jnp.int32, (8, SIDE), 0)
+    return jnp.concatenate([jnp.where(row == 0, first[:8], rest[:8]), rest[8:]], axis=0)
+
+
+def unfold(real, imag):
+    (tr, br), (ti, bi) = halves(real), halves(imag)
+    return (
+        jnp.concatenate([with_first_row(tr, tr + bi), with_first_row(br, tr - bi)], axis=0),
+        jnp.concatenate([with_first_row(ti, ti - br), with_first_row(bi, ti + br)], axis=0),
+    )
+
+
+def fold(real, imag):
+    (tr, br), (ti, bi) = halves(real), halves(imag)
+    return (
+        jnp.concatenate([with_first_row(tr, tr + br), with_first_row(br, bi - ti)], axis=0),
+        jnp.concatenate([with_first_row(ti, ti + bi), with_first_row(bi, tr - br)], axis=0),
+    )
+
+
+def to_frequency(waves, fields):
+    for turn in (True, False):
+        planes = multiply(waves[0], [plane for field in fields for plane in field])
+        yield
+        fields = [unfold(*planes[k : k + 2]) for k in range(0, len(planes), 2)]
+        if turn:
+            fields = [(real.T, imag.T) for real, imag in fields]
+    return fields
+
+
+def from_frequency(waves, fields):
+    for turn in (True, False):
+        planes = multiply(waves[1], [plane for field in fields for plane in fold(*field)])
+        yield
+        if turn:
+            planes = [plane.T for plane in planes]
+        fields = [tuple(planes[k : k + 2]) for k in range(0, len(planes), 2)]
+    return fields
+
+
+def product(left, right):
+    return left[0] * right[0] - left[1] * right[1], left[0] * right[1] + left[1] * right[0]
+
+
+def conjugate_product(left, right):
+    return left[0] * right[0] + left[1] * right[1], left[0] * right[1] - left[1] * right[0]
+
+
+def grads_kernel(field, amp, meta_hbm, probe, prop_ref, waves_hbm, packed, grad, waves, meta_ref, order, sems):
     core = lax.axis_index("pos") % 2
     base = 6 * core
     meta_load = pltpu.make_async_copy(meta_hbm, meta_ref, sems.at[0])
     meta_load.start()
-    left_load = pltpu.make_async_copy(left_hbm, left_ref, sems.at[1])
-    left_load.start()
-    right_load = pltpu.make_async_copy(right_hbm, right_ref, sems.at[2])
-    right_load.start()
-
-    def widen(index, _):
-        plane, block = index // SPAN, index % SPAN
-        inside = block + base - 8 * core
-        within = (inside >= 0) & (inside < 8)
-        extra = block + base - (8 - 2 * core)
-        part = jnp.where(within, inside // 2, plane)
-        tile = jnp.where(within, plane * 2 + inside % 2, 8 + extra)
-        span = pl.ds(pl.multiple_of((base + block) * SIDE, SIDE), SIDE)
-        field[plane, block, :SIDE, :] = obj_ref[plane, :, span].astype(jnp.bfloat16).astype(jnp.float32)
-        field[plane, block, SIDE:, :] = halo[part, tile].astype(jnp.float32)
-        grad[block, plane] = jnp.zeros((2 * SIDE, SIDE), jnp.float32)
-        return 0
-
-    lax.fori_loop(0, 4 * SPAN, widen, 0)
-    prop_ref[0] = jnp.cos(phase[...])
-    prop_ref[1] = jnp.sin(phase[...])
+    waves_load = pltpu.make_async_copy(waves_hbm, waves, sems.at[1])
+    waves_load.start()
+
+    def clear(block, _):
+        grad[block] = jnp.zeros((4, 2 * SIDE, SIDE), jnp.float32)
+        return 0
+
+    lax.fori_loop(0, SPAN, clear, 0)
     meta_load.wait()
-    left_load.wait()
-    right_load.wait()
+    waves_load.wait()
 
     def read(slot):
         code = meta_ref[slot // 32, slot % 32 // 2, 0, slot % 2] - 1
@@ -148,32 +171,27 @@
         grad[block, plane, rows, :] += jnp.where(lane >= shift, moved, zero)
         grad[next_block, plane, rows, :] += jnp.where(lane < shift, moved, zero)
 
-    def pair(parts):
-        return jnp.concatenate(parts, axis=1)
-
-    forward = (left_ref, right_ref, 0)
-    inverse = (left_ref, right_ref, 1)
-
     def stages(where, slot, weight):
-        t0r, t1r, t0i, t1i = [pair([cut(plane, where)] * 2) for plane in range(4)]
-        pr, pi = [pair([probe[0, k], probe[1, k]]) for k in range(2)]
-        kr, ki = [pair([prop_ref[k]] * 2) for k in range(2)]
-        wr, wi = pr * t0r - pi * t0i, pr * t0i + pi * t0r
+        t0, t1 = [(cut(k, where), cut(k + 2, where)) for k in range(2)]
+        probes = [(probe[m, 0], probe[m, 1]) for m in range(2)]
+        prop = (prop_ref[0], prop_ref[1])
+        fields = [product(p, t0) for p in probes]
         yield
-        sr, si = yield from transform2d(*forward, wr, wi)
-        ur, ui = yield from transform2d(*inverse, sr * kr - si * ki, sr * ki + si * kr)
-        fr, fi = yield from transform2d(*forward, ur * t1r - ui * t1i, ur * t1i + ui * t1r)
-        power = fr * fr + fi * fi
-        model = 1.0 + power[:, :SIDE] + power[:, SIDE:]
-        amplitude = decoded(amp[slot // 32, slot % 32 // 2, slot % 2])
-        factor = pair([weight * (1.0 - amplitude * lax.rsqrt(model))] * 2)
-        gr, gi = yield from transform2d(*inverse, fr * factor, fi * factor)
-        for plane, value in ((1, ur * gr + ui * gi), (3, ur * gi - ui * gr)):
-            add(plane, where, value[:, :SIDE] + value[:, SIDE:])
-        hr, hi = yield from transform2d(*forward, t1r * gr + t1i * gi, t1r * gi - t1i * gr)
-        er, ei = yield from transform2d(*inverse, kr * hr + ki * hi, kr * hi - ki * hr)
-        for plane, value in ((0, pr * er + pi * ei), (2, pr * ei - pi * er)):
-            add(plane, where, value[:, :SIDE] + value[:, SIDE:])
+        fields = yield from to_frequency(waves, fields)
+        middle = yield from from_frequency(waves, [product(f, prop) for f in fields])
+        far = yield from to_frequency(waves, [product(u, t1) for u in middle])
+        model = 1.0 + sum(real * real + imag * imag for real, imag in far)
+        factor = weight * (1.0 - decoded(amp[slot // 32, slot % 32 // 2, slot % 2]) * lax.rsqrt(model))
+        fields = yield from from_frequency(waves, [(real * factor, imag * factor) for real, imag in far])
+
+        def add_slice(k, parts):
+            add(k, where, parts[0][0] + parts[1][0])
+            add(k + 2, where, parts[0][1] + parts[1][1])
+
+        add_slice(1, [conjugate_product(u, g) for u, g in zip(middle, fields)])
+        fields = yield from to_frequency(waves, [conjugate_product(t1, g) for g in fields])
+        fields = yield from from_frequency(waves, [conjugate_product(prop, h) for h in fields])
+        add_slice(0, [conjugate_product(p, e) for p, e in zip(probes, fields)])
 
     def step(groups, start, index, _):
         running = []
@@ -198,32 +216,28 @@
     lax.fori_loop(0, SPAN, pack, 0)
 
 
-def grads_call(obj, halo, amp, meta, probe, phase):
-    left, right = [pltpu.with_memory_space_constraint(jnp.asarray(x), pltpu.HBM) for x in dft_operands()]
+def grads_call(field, amp, meta, probe, prop, waves):
     hbm = pl.BlockSpec(memory_space=pltpu.HBM)
     vmem = pl.BlockSpec(memory_space=pltpu.VMEM)
     return pl.pallas_call(
         grads_kernel,
         out_shape=jax.ShapeDtypeStruct((SPAN, 4, 2 * SIDE, SIDE), jnp.bfloat16),
-        in_specs=[vmem] * 6 + [hbm] * 2,
+        in_specs=[vmem] * 5 + [hbm],
         out_specs=vmem,
         scratch_shapes=[
-            pltpu.VMEM((4, SPAN, 2 * SIDE, SIDE), jnp.float32),
             pltpu.VMEM((SPAN, 4, 2 * SIDE, SIDE), jnp.float32),
-            pltpu.VMEM((2, SIDE, SIDE), jnp.float32),
-            pltpu.VMEM(left.shape, jnp.bfloat16),
-            pltpu.VMEM(right.shape, jnp.bfloat16),
+            pltpu.VMEM(waves.shape, jnp.bfloat16),
             pltpu.SMEM(meta.shape, jnp.int32),
             pltpu.SMEM((65,), jnp.int32),
-            pltpu.SemaphoreType.DMA((3,)),
+            pltpu.SemaphoreType.DMA((2,)),
         ],
         compiler_params=pltpu.CompilerParams(vmem_limit_bytes=K2_LIMIT * 2**20),
         name="window_gradients",
-    )(obj, halo, amp, meta, probe, phase, left, right)
-
-
-def send_kernel(obj_ref, measured_ref, offsets_ref, halo_ref, amp_ref, meta_ref,
-                wide, extra, measured, chunk, amp_out, meta_out, local_sem, halo_send, halo_recv, amp_send, amp_recv, meta_send, meta_recv, twin_send, twin_recv):
+    )(field, amp, meta, probe, prop, pltpu.with_memory_space_constraint(waves, pltpu.HBM))
+
+
+def send_kernel(obj_ref, measured_ref, phase_hbm, turn_hbm, offsets_ref, field, amp_ref, meta_ref, prop_ref,
+                wide, extra, measured, own, phase, turn, halo_ref, codes_ref, chunk, amp_out, meta_out, local_sem, halo_send, halo_recv, amp_send, amp_recv, meta_send, meta_recv, twin_send, twin_recv):
     strip, pos = lax.axis_index("obj"), lax.axis_index("pos")
     x, core = pos // 2, pos % 2
     twin = (strip, x * 2 + 1 - core)
@@ -235,6 +249,9 @@
         pltpu.make_async_copy(obj_ref.at[:, :, span(8 * core + 2 * x)], wide, local_sem.at[0]),
         pltpu.make_async_copy(obj_ref.at[x, :, span(8 - 2 * core)], extra, local_sem.at[1]),
         pltpu.make_async_copy(measured_ref, measured, local_sem.at[2]),
+        pltpu.make_async_copy(turn_hbm, turn, local_sem.at[3]),
+        pltpu.make_async_copy(phase_hbm, phase, local_sem.at[4]),
+        pltpu.make_async_copy(obj_ref.at[:, :, pl.ds(pl.multiple_of(6 * core * SIDE, SIDE), SPAN * SIDE)], own, local_sem.at[5]),
     ]
     for load in loads:
         load.start()
@@ -297,6 +314,24 @@
 
     lane = lax.broadcasted_iota(jnp.int32, META_TILE, 1)
     loads[2].wait()
+    loads[3].wait()
+    turn_back = turn[...].astype(jnp.float32).T.astype(jnp.bfloat16)
+
+    def reorder(planes):
+        rows = jnp.dot(jnp.concatenate(planes, axis=0).astype(jnp.bfloat16), turn_back, preferred_element_type=jnp.float32)
+        rows = [rows[k * SIDE : (k + 1) * SIDE].T for k in range(len(planes))]
+        rows = jnp.dot(jnp.concatenate(rows, axis=0).astype(jnp.bfloat16), turn_back, preferred_element_type=jnp.float32)
+        return [rows[k * SIDE : (k + 1) * SIDE] for k in range(len(planes))]
+
+    def encode(group, _):
+        codes = [coded(measured[4 * group + k]) for k in range(4)]
+        high = [jnp.floor(code * (1.0 / 256.0)) for code in codes]
+        planes = reorder(high + [code - 256.0 * part for code, part in zip(codes, high)])
+        for k in range(4):
+            codes_ref[4 * group + k] = (256.0 * planes[k] + planes[4 + k]).astype(jnp.int32).astype(AMP)
+        return 0
+
+    lax.fori_loop(0, measured.shape[0] // 4, encode, 0)
 
     def packed(target):
         where, codes, seen = [jnp.int32(0)] * CAP, [jnp.int32(0)] * CAP, jnp.int32(0)
@@ -308,7 +343,7 @@
                 where[k] = jnp.where(take, item, where[k])
                 codes[k] = jnp.where(take, 1 + row % SIDE * 2048 + col, codes[k])
             seen = seen + here.astype(jnp.int32)
-        return jnp.where(lane == 0, codes[0], codes[1]), [coded(measured[index]) for index in where]
+        return jnp.where(lane == 0, codes[0], codes[1]), [codes_ref[index] for index in where]
 
     def pack(step, _):
         target = lax.rem(strip + step, 16)
@@ -336,6 +371,25 @@
         amp_ref[core, strip, k] = values[k]
     to_twin(strip, core).start()
 
+    loads[4].wait()
+    value, planes = phase[...], []
+    for _ in range(3):
+        planes.append(value.astype(jnp.bfloat16))
+        value = value - planes[-1].astype(jnp.float32)
+    planes = reorder(planes)
+    moved_phase = planes[0] + planes[1] + planes[2]
+    prop_ref[0] = jnp.cos(moved_phase)
+    prop_ref[1] = jnp.sin(moved_phase)
+    loads[5].wait()
+
+    def widen_own(block, _):
+        span = pl.ds(pl.multiple_of(block * SIDE, SIDE), SIDE)
+        for plane in range(4):
+            field[plane, block, :SIDE, :] = own[plane, :, span].astype(jnp.bfloat16).astype(jnp.float32)
+        return 0
+
+    lax.fori_loop(0, SPAN, widen_own, 0)
+
     def relay(step, _):
         source = lax.rem(strip + 16 - step, 16)
         amp_copy(source, source).wait_recv()
@@ -365,31 +419,50 @@
     for number in range(PIECES):
         for step in range(1, 4):
             spread(chunk, lax.rem(x + step, 4), number, (strip, pos), 0).wait_recv()
+
+    def widen_halo(step, _):
+        part = step // 2
+        block = 2 * core + step
+        for plane in range(4):
+            field[plane, block, SIDE:, :] = halo_ref[part, 2 * plane + step % 2].astype(jnp.float32)
+        return 0
+
+    lax.fori_loop(0, 8, widen_halo, 0)
+    for plane in range(4):
+        for block in range(2):
+            field[plane, 8 - 8 * core + block, SIDE:, :] = halo_ref[plane, 8 + block].astype(jnp.float32)
+    for number in range(PIECES):
         for step in range(4):
             spread(chunk, x, number, (strip, pos), step).wait_send()
 
 
-def send_call(obj, measured, offsets):
+def send_call(obj, measured, phase, order, offsets):
     hbm = pl.BlockSpec(memory_space=pltpu.HBM)
     vmem = pl.BlockSpec(memory_space=pltpu.VMEM)
     dma = pltpu.SemaphoreType.DMA
     return pl.pallas_call(
         send_kernel,
         out_shape=(
-            jax.ShapeDtypeStruct((4, 10, SIDE, SIDE), jnp.bfloat16),
+            jax.ShapeDtypeStruct((4, SPAN, 2 * SIDE, SIDE), jnp.float32),
             jax.ShapeDtypeStruct((2, 16, CAP, SIDE, SIDE), AMP),
             jax.ShapeDtypeStruct((2, 16, *META_TILE), jnp.int32),
+            jax.ShapeDtypeStruct((2, SIDE, SIDE), jnp.float32),
         ),
-        in_specs=[hbm, hbm, pl.BlockSpec(memory_space=pltpu.SMEM)],
-        out_specs=(vmem, vmem, vmem),
+        in_specs=[hbm] * 4 + [pl.BlockSpec(memory_space=pltpu.SMEM)],
+        out_specs=(vmem,) * 4,
         scratch_shapes=[
             pltpu.VMEM((4, SIDE, 2 * SIDE), jnp.float32),
             pltpu.VMEM((SIDE, 2 * SIDE), jnp.float32),
             pltpu.VMEM(measured.shape, jnp.float32),
+            pltpu.VMEM((4, SIDE, SPAN * SIDE), jnp.float32),
+            pltpu.VMEM((SIDE, SIDE), jnp.float32),
+            pltpu.VMEM((SIDE, SIDE), jnp.bfloat16),
+            pltpu.VMEM((4, 10, SIDE, SIDE), jnp.bfloat16),
+            pltpu.VMEM(measured.shape, AMP),
             pltpu.VMEM((10, SIDE, SIDE), jnp.bfloat16),
             pltpu.VMEM((16, CAP, SIDE, SIDE), AMP),
             pltpu.VMEM((16, *META_TILE), jnp.int32),
-            dma((3,)),
+            dma((6,)),
             dma((4, PIECES)),
             dma((4, PIECES)),
             dma((16,)),
@@ -399,11 +472,9 @@
             dma((17,)),
             dma((17,)),
         ],
-        compiler_params=pltpu.CompilerParams(collective_id=0, has_side_effects=True, vmem_limit_bytes=16 * 2**20),
+        compiler_params=pltpu.CompilerParams(collective_id=0, has_side_effects=True, vmem_limit_bytes=20 * 2**20),
         name="exchange_inputs",
-    )(
-        pltpu.with_memory_space_constraint(obj, pltpu.HBM), pltpu.with_memory_space_constraint(measured, pltpu.HBM), offsets
-    )
+    )(*[pltpu.with_memory_space_constraint(x, pltpu.HBM) for x in (obj, measured, phase, order)], offsets)
 
 
 def sum_kernel(grad_ref, out_ref, theirs, joined, parts, low_in, low_out, twin_send, twin_recv, x_send, x_recv, low_send, low_recv):
@@ -525,8 +596,9 @@
 
 def per_device(object_field, probe_modes, propagator_phase, offsets, measured):
     obj = object_field.reshape(4, SIDE, object_field.shape[3])
-    halo, amp, meta = send_call(obj, measured, offsets.T)
-    grad = grads_call(obj, halo, amp, meta, probe_modes, propagator_phase)
+    waves, order = [jnp.asarray(x) for x in dft_operands()]
+    field, amp, meta, prop = send_call(obj, measured, propagator_phase, order, offsets.T)
+    grad = grads_call(field, amp, meta, probe_modes, prop, waves)
     return sum_call(grad).reshape(2, 2, SIDE, 2 * SIDE)
 
 

time: 96.9 us -> 95.1 us (0.981)
  the two profiles are of different devices: /device:TPU:1 before, /device:TPU:11 now
where the time goes in v4:
time: 95.1 us; the launch traced here: 95 us
  Pallas kernels  93.4 us (98%)
  local copies, waits for them, and re-layouts  1.52 us (2%)
    pallas_call x1, Pallas kernels, sum_call(): pl.pallas_call(sum_kernel, out_shape=jax.ShapeDtypeStruct((4, SIDE, 2 * S...  34.5 us
    pallas_call x1, Pallas kernels, send_call(): pl.pallas_call(send_kernel, out_shape=(jax.ShapeDtypeStruct((4, SPAN, 2 *...  31.1 us
    pallas_call x1, Pallas kernels, grads_call(): pl.pallas_call(grads_kernel, out_shape=jax.ShapeDtypeStruct((SPAN, 4, 2 *...  27.9 us

profile of v4, /device:TPU:11, one launch (start us, length us, event | category | flops | bytes accessed | tf_op | source)
XLA Modules:
  0.0 95.0 jit_solution(15241538172690379321)
XLA Ops:
  0.0 0.0 copy-start
  0.0 0.0 copy-start.1
  0.0 0.7 copy-done.1
  0.7 31.1 %exchange_inputs.1 = (f32[4,10,256,128]{3,2,1,0:T(8,128)S(1)}, s16[2,16,2,128,128]{4,3,2,1,0:T(8,128)(2,1)S(1)}, s32[2,16,1,128]{3,2,1,0:T(1,128)S(1)}, f32[2,128,128]{2,1,0:T(8,128)S(1)}) custom-call(f32[4,128,2048]{2,1,0:T(8,128)} %bitcast.5, f32[16,128,128]{2,1,0:T(8,128)} %measured_ref.1, f32[128,128]{1,0:T(8,128)} %phase_hbm.1, ...), custom_call_target="tpu_custom_call" | custom-call | tf_op jit(solution)/shard_map/exchange_inputs/pallas_call | solution.py:443
  31.8 0.0 copy-done
  31.8 27.9 %window_gradients.1.grad_ref = bf16[10,4,256,128]{3,2,1,0:T(8,128)(2,1)S(1)} custom-call(f32[4,10,256,128]{3,2,1,0:T(8,128)S(1)} %get-tuple-element.9.field, s16[2,16,2,128,128]{4,3,2,1,0:T(8,128)(2,1)S(1)} %get-tuple-element.10.amp, s32[2,16,1,128]{3,2,1,0:T(1,128)S(1)} %get-tuple-element.11.meta_hbm, f32[2,2,128,128]{3,2,1,0:T(8,128)S(1)} %copy-done, ...), custom_call_target="tpu_custom_call" | custom-call | tf_op jit(solution)/shard_map/window_gradients/pallas_call | solution.py:222
  59.7 34.5 %sum_gradients.1 = f32[4,128,256]{2,1,0:T(8,128)S(1)} custom-call(bf16[10,4,256,128]{3,2,1,0:T(8,128)(2,1)S(1)} %window_gradients.1.grad_ref), custom_call_target="tpu_custom_call" | custom-call | tf_op jit(solution)/shard_map/sum_gradients/pallas_call | solution.py:574
  94.2 0.8 copy.9
Async XLA Ops:
  0.0 31.8 %copy-start = (f32[2,2,128,128]{3,2,1,0:T(8,128)S(1)}, f32[2,2,128,128]{3,2,1,0:T(8,128)}, u32[]{:S(2)}) copy-start(f32[2,2,128,128]{3,2,1,0:T(8,128)} %probe.1) | copy-start | bytes 786436
  0.0 0.7 copy-start.1

commit v5 on v4

--- a/solution.py
+++ b/solution.py
@@ -12,7 +12,8 @@
 CAP = 2
 SIDE = 128
 META_TILE = (1, 128)
-PIECES = 5
+PIECES = 4
+CHAINS, LAST_CHAINS = 5, 3
 K2_LIMIT = 30
 SPAN = 10
 LOW_COL, HIGH_COL = 768, 1152
@@ -116,13 +117,7 @@
     waves_load = pltpu.make_async_copy(waves_hbm, waves, sems.at[1])
     waves_load.start()
 
-    def clear(block, _):
-        grad[block] = jnp.zeros((4, 2 * SIDE, SIDE), jnp.float32)
-        return 0
-
-    lax.fori_loop(0, SPAN, clear, 0)
     meta_load.wait()
-    waves_load.wait()
 
     def read(slot):
         code = meta_ref[slot // 32, slot % 32 // 2, 0, slot % 2] - 1
@@ -135,7 +130,15 @@
         last = here * (col > HIGH_COL).astype(jnp.int32)
         return counts[0] + here, counts[1] + first, counts[2] + last
 
-    whole, first_only, last_only = lax.fori_loop(0, 64, tally, (0, 0, 0), unroll=8)
+    def tally_and_clear(index, counts):
+        for k in range(8):
+            counts = tally(8 * index + k, counts)
+        for k in range(SPAN // 2):
+            tile = SPAN // 2 * index + k
+            grad[tile // 4, tile % 4] = jnp.zeros((2 * SIDE, SIDE), jnp.float32)
+        return counts
+
+    whole, first_only, last_only = lax.fori_loop(0, 8, tally_and_clear, (0, 0, 0))
     either = whole - first_only - last_only
     to_first = jnp.clip((whole + 1) // 2 - first_only, 0, either)
 
@@ -149,6 +152,7 @@
         return count + mine.astype(jnp.int32), seen + (valid & free).astype(jnp.int32)
 
     count, _ = lax.fori_loop(0, 64, collect, (0, 0), unroll=8)
+    waves_load.wait()
     lane = lax.broadcasted_iota(jnp.int32, (SIDE, SIDE), 1)
 
     def place(slot):
@@ -204,10 +208,10 @@
             running = [machine for machine in running if next(machine, 0) is None]
         return 0
 
-    fours = (count + 1) // 4
-    lax.fori_loop(0, fours, functools.partial(step, 4, 0), 0)
-    rest = jnp.clip((count - 4 * fours + 1) // 2, 0, 1)
-    lax.fori_loop(0, rest, functools.partial(step, 2, 4 * fours), 0)
+    full = (count + CHAINS - 1 - LAST_CHAINS) // CHAINS
+    lax.fori_loop(0, full, functools.partial(step, CHAINS, 0), 0)
+    rest = jnp.clip(count - CHAINS * full, 0, 1)
+    lax.fori_loop(0, rest, functools.partial(step, LAST_CHAINS, CHAINS * full), 0)
 
     def pack(block, _):
         packed[block] = grad[block].astype(jnp.bfloat16)
@@ -237,7 +241,7 @@
 
 
 def send_kernel(obj_ref, measured_ref, phase_hbm, turn_hbm, offsets_ref, field, amp_ref, meta_ref, prop_ref,
-                wide, extra, measured, own, phase, turn, halo_ref, codes_ref, chunk, amp_out, meta_out, local_sem, halo_send, halo_recv, amp_send, amp_recv, meta_send, meta_recv, twin_send, twin_recv):
+                wide, measured, own, phase, turn, halo_ref, codes_ref, chunk, amp_out, meta_out, local_sem, halo_send, halo_recv, shared_sem, slot_sem, twin_sem):
     strip, pos = lax.axis_index("obj"), lax.axis_index("pos")
     x, core = pos // 2, pos % 2
     twin = (strip, x * 2 + 1 - core)
@@ -247,11 +251,10 @@
 
     loads = [
         pltpu.make_async_copy(obj_ref.at[:, :, span(8 * core + 2 * x)], wide, local_sem.at[0]),
-        pltpu.make_async_copy(obj_ref.at[x, :, span(8 - 2 * core)], extra, local_sem.at[1]),
-        pltpu.make_async_copy(measured_ref, measured, local_sem.at[2]),
-        pltpu.make_async_copy(turn_hbm, turn, local_sem.at[3]),
-        pltpu.make_async_copy(phase_hbm, phase, local_sem.at[4]),
-        pltpu.make_async_copy(obj_ref.at[:, :, pl.ds(pl.multiple_of(6 * core * SIDE, SIDE), SPAN * SIDE)], own, local_sem.at[5]),
+        pltpu.make_async_copy(measured_ref, measured, local_sem.at[1]),
+        pltpu.make_async_copy(turn_hbm, turn, local_sem.at[2]),
+        pltpu.make_async_copy(phase_hbm, phase, local_sem.at[3]),
+        pltpu.make_async_copy(obj_ref.at[:, :, pl.ds(pl.multiple_of(6 * core * SIDE, SIDE), SPAN * SIDE)], own, local_sem.at[4]),
     ]
     for load in loads:
         load.start()
@@ -267,16 +270,14 @@
         pl.semaphore_signal(barrier, inc=1, device_id=(strip, other), device_id_type=MESH)
     pl.semaphore_signal(barrier, inc=1, device_id=twin, device_id_type=MESH)
     loads[0].wait()
-    loads[1].wait()
     for block in range(2):
         lanes = slice(block * SIDE, (block + 1) * SIDE)
         for plane in range(4):
             chunk[plane * 2 + block] = wide[plane, :, lanes].astype(jnp.bfloat16)
-        chunk[8 + block] = extra[:, lanes].astype(jnp.bfloat16)
     pl.semaphore_wait(barrier, 19)
 
     def piece(number):
-        return pl.ds(number * (10 // PIECES), 10 // PIECES)
+        return pl.ds(number * (8 // PIECES), 8 // PIECES)
 
     def spread(source, index, number, where, send):
         return pltpu.make_async_remote_copy(
@@ -288,33 +289,40 @@
     for number in range(PIECES):
         spread(chunk, x, number, above, 0).start()
 
-    def amp_copy(target, source):
+    def amp_copy(target):
         return pltpu.make_async_remote_copy(
-            src_ref=amp_out.at[target], dst_ref=amp_ref.at[core, source], send_sem=amp_send.at[target],
-            recv_sem=amp_recv.at[source], device_id=(target, pos), device_id_type=MESH,
+            src_ref=amp_out.at[target], dst_ref=amp_ref.at[core, strip], send_sem=slot_sem.at[0],
+            recv_sem=slot_sem.at[1], device_id=(target, pos), device_id_type=MESH,
         )
 
-    def meta_copy(target, source):
+    def meta_copy(target):
         return pltpu.make_async_remote_copy(
-            src_ref=meta_out.at[target], dst_ref=meta_ref.at[core, source], send_sem=meta_send.at[target],
-            recv_sem=meta_recv.at[source], device_id=(target, pos), device_id_type=MESH,
+            src_ref=meta_out.at[target], dst_ref=meta_ref.at[core, strip], send_sem=slot_sem.at[2],
+            recv_sem=slot_sem.at[3], device_id=(target, pos), device_id_type=MESH,
         )
 
-    def to_twin(source, side):
-        return pltpu.make_async_remote_copy(
-            src_ref=amp_ref.at[core, source], dst_ref=amp_ref.at[side, source], send_sem=twin_send.at[source],
-            recv_sem=twin_recv.at[source], device_id=twin, device_id_type=MESH,
-        )
-
-    def meta_to_twin(side):
-        return pltpu.make_async_remote_copy(
-            src_ref=meta_ref.at[core], dst_ref=meta_ref.at[side], send_sem=twin_send.at[16],
-            recv_sem=twin_recv.at[16], device_id=twin, device_id_type=MESH,
-        )
+    def all_copies():
+        others = pl.ds(0, 15)
+        return [
+            pltpu.make_async_remote_copy(
+                src_ref=source.at[others], dst_ref=target.at[core, others], send_sem=slot_sem.at[2 * k],
+                recv_sem=slot_sem.at[2 * k + 1], device_id=twin, device_id_type=MESH,
+            )
+            for k, (source, target) in enumerate(((amp_out, amp_ref), (meta_out, meta_ref)))
+        ]
+
+    def to_twin(side):
+        return [
+            pltpu.make_async_remote_copy(
+                src_ref=ref.at[core], dst_ref=ref.at[side], send_sem=twin_sem.at[2 * k], recv_sem=twin_sem.at[2 * k + 1],
+                device_id=twin, device_id_type=MESH,
+            )
+            for k, ref in enumerate((amp_ref, meta_ref))
+        ]
 
     lane = lax.broadcasted_iota(jnp.int32, META_TILE, 1)
+    loads[1].wait()
     loads[2].wait()
-    loads[3].wait()
     turn_back = turn[...].astype(jnp.float32).T.astype(jnp.bfloat16)
 
     def reorder(planes):
@@ -346,13 +354,13 @@
         return jnp.where(lane == 0, codes[0], codes[1]), [codes_ref[index] for index in where]
 
     def pack(step, _):
-        target = lax.rem(strip + step, 16)
+        target = (strip // 4 + step % 4) % 4 * 4 + (strip + step // 4) % 4
         codes, values = packed(target)
         meta_out[target] = codes
         for k in range(CAP):
             amp_out[target, k] = values[k]
-        amp_copy(target, strip).start()
-        meta_copy(target, strip).start()
+        amp_copy(target).start()
+        meta_copy(target).start()
         return 0
 
     def forward(number):
@@ -361,17 +369,15 @@
             spread(halo_ref.at[x], x, number, (strip, lax.rem(x + step, 4) * 2 + core), step).start()
 
     bounds = [1, 6] + [6 + (10 * k) // PIECES for k in range(1, PIECES)] + [16]
-    lax.fori_loop(bounds[0], bounds[1], pack, 0)
+    lax.fori_loop(1, 16, pack, 0)
     for number in range(PIECES):
         forward(number)
-        lax.fori_loop(bounds[number + 1], bounds[number + 2], pack, 0)
     codes, values = packed(strip)
     meta_ref[core, strip] = codes
     for k in range(CAP):
         amp_ref[core, strip, k] = values[k]
-    to_twin(strip, core).start()
-
-    loads[4].wait()
+
+    loads[3].wait()
     value, planes = phase[...], []
     for _ in range(3):
         planes.append(value.astype(jnp.bfloat16))
@@ -380,7 +386,7 @@
     moved_phase = planes[0] + planes[1] + planes[2]
     prop_ref[0] = jnp.cos(moved_phase)
     prop_ref[1] = jnp.sin(moved_phase)
-    loads[5].wait()
+    loads[4].wait()
 
     def widen_own(block, _):
         span = pl.ds(pl.multiple_of(block * SIDE, SIDE), SIDE)
@@ -390,35 +396,21 @@
 
     lax.fori_loop(0, SPAN, widen_own, 0)
 
-    def relay(step, _):
-        source = lax.rem(strip + 16 - step, 16)
-        amp_copy(source, source).wait_recv()
-        meta_copy(source, source).wait_recv()
-        to_twin(source, core).start()
-        return 0
-
-    lax.fori_loop(1, 16, relay, 0)
-    meta_to_twin(core).start()
-
-    def finish(step, _):
-        target = lax.rem(strip + step, 16)
-        amp_copy(target, strip).wait_send()
-        meta_copy(target, strip).wait_send()
-        return 0
-
-    lax.fori_loop(1, 16, finish, 0)
-
-    def finish_twin(source, _):
-        to_twin(source, core).wait_send()
-        to_twin(source, 1 - core).wait_recv()
-        return 0
-
-    lax.fori_loop(0, 16, finish_twin, 0)
-    meta_to_twin(core).wait_send()
-    meta_to_twin(1 - core).wait_recv()
+    arrivals = all_copies()
+    for copy in arrivals:
+        copy.wait_recv()
+    relays = to_twin(core)
+    for copy in relays:
+        copy.start()
     for number in range(PIECES):
         for step in range(1, 4):
             spread(chunk, lax.rem(x + step, 4), number, (strip, pos), 0).wait_recv()
+
+    shared = pltpu.make_async_remote_copy(
+        src_ref=halo_ref.at[3 - 3 * core], dst_ref=halo_ref.at[4], send_sem=shared_sem.at[0], recv_sem=shared_sem.at[1],
+        device_id=twin, device_id_type=MESH,
+    )
+    shared.start()
 
     def widen_halo(step, _):
         part = step // 2
@@ -428,9 +420,14 @@
         return 0
 
     lax.fori_loop(0, 8, widen_halo, 0)
+    shared.wait()
     for plane in range(4):
         for block in range(2):
-            field[plane, 8 - 8 * core + block, SIDE:, :] = halo_ref[plane, 8 + block].astype(jnp.float32)
+            field[plane, 8 - 8 * core + block, SIDE:, :] = halo_ref[4, 2 * plane + block].astype(jnp.float32)
+    for copy in arrivals + relays:
+        copy.wait_send()
+    for copy in to_twin(1 - core):
+        copy.wait_recv()
     for number in range(PIECES):
         for step in range(4):
             spread(chunk, x, number, (strip, pos), step).wait_send()
@@ -452,25 +449,21 @@
         out_specs=(vmem,) * 4,
         scratch_shapes=[
             pltpu.VMEM((4, SIDE, 2 * SIDE), jnp.float32),
-            pltpu.VMEM((SIDE, 2 * SIDE), jnp.float32),
             pltpu.VMEM(measured.shape, jnp.float32),
             pltpu.VMEM((4, SIDE, SPAN * SIDE), jnp.float32),
             pltpu.VMEM((SIDE, SIDE), jnp.float32),
             pltpu.VMEM((SIDE, SIDE), jnp.bfloat16),
-            pltpu.VMEM((4, 10, SIDE, SIDE), jnp.bfloat16),
+            pltpu.VMEM((5, 8, SIDE, SIDE), jnp.bfloat16),
             pltpu.VMEM(measured.shape, AMP),
-            pltpu.VMEM((10, SIDE, SIDE), jnp.bfloat16),
+            pltpu.VMEM((8, SIDE, SIDE), jnp.bfloat16),
             pltpu.VMEM((16, CAP, SIDE, SIDE), AMP),
             pltpu.VMEM((16, *META_TILE), jnp.int32),
-            dma((6,)),
+            dma((5,)),
             dma((4, PIECES)),
             dma((4, PIECES)),
-            dma((16,)),
-            dma((16,)),
-            dma((16,)),
-            dma((16,)),
-            dma((17,)),
-            dma((17,)),
+            dma((2,)),
+            dma((4,)),
+            dma((4,)),
         ],
         compiler_params=pltpu.CompilerParams(collective_id=0, has_side_effects=True, vmem_limit_bytes=20 * 2**20),
         name="exchange_inputs",

time: 95.1 us -> 88 us (0.925)
  the two profiles are of different devices: /device:TPU:11 before, /device:TPU:1 now
where the time goes in v5:
time: 88 us; the launch traced here: 87.9 us
  Pallas kernels  86.3 us (98%)
  local copies, waits for them, and re-layouts  1.52 us (2%)
    pallas_call x1, Pallas kernels, send_call(): pl.pallas_call(send_kernel, out_shape=(jax.ShapeDtypeStruct((4, SPAN, 2 *...  30.1 us
    pallas_call x1, Pallas kernels, sum_call(): pl.pallas_call(sum_kernel, out_shape=jax.ShapeDtypeStruct((4, SIDE, 2 * S...  29.1 us
    pallas_call x1, Pallas kernels, grads_call(): pl.pallas_call(grads_kernel, out_shape=jax.ShapeDtypeStruct((SPAN, 4, 2 *...  27.2 us

profile of v5, /device:TPU:1, one launch (start us, length us, event | category | flops | bytes accessed | tf_op | source)
XLA Modules:
  0.0 87.9 jit_solution(5003733564574242813)
XLA Ops:
  0.0 0.0 copy-start
  0.0 0.0 copy-start.1
  0.0 0.7 copy-done.1
  0.7 30.1 %exchange_inputs.1 = (f32[4,10,256,128]{3,2,1,0:T(8,128)S(1)}, s16[2,16,2,128,128]{4,3,2,1,0:T(8,128)(2,1)S(1)}, s32[2,16,1,128]{3,2,1,0:T(1,128)S(1)}, f32[2,128,128]{2,1,0:T(8,128)S(1)}) custom-call(f32[4,128,2048]{2,1,0:T(8,128)} %bitcast.5, f32[16,128,128]{2,1,0:T(8,128)} %measured_ref.1, f32[128,128]{1,0:T(8,128)} %phase_hbm.1, ...), custom_call_target="tpu_custom_call" | custom-call | tf_op jit(solution)/shard_map/exchange_inputs/pallas_call | solution.py:440
  30.9 0.0 copy-done
  30.9 27.2 %window_gradients.1.grad_ref = bf16[10,4,256,128]{3,2,1,0:T(8,128)(2,1)S(1)} custom-call(f32[4,10,256,128]{3,2,1,0:T(8,128)S(1)} %get-tuple-element.9.field, s16[2,16,2,128,128]{4,3,2,1,0:T(8,128)(2,1)S(1)} %get-tuple-element.10.amp, s32[2,16,1,128]{3,2,1,0:T(1,128)S(1)} %get-tuple-element.11.meta_hbm, f32[2,2,128,128]{3,2,1,0:T(8,128)S(1)} %copy-done, ...), custom_call_target="tpu_custom_call" | custom-call | tf_op jit(solution)/shard_map/window_gradients/pallas_call | solution.py:226
  58.0 29.1 %sum_gradients.1 = f32[4,128,256]{2,1,0:T(8,128)S(1)} custom-call(bf16[10,4,256,128]{3,2,1,0:T(8,128)(2,1)S(1)} %window_gradients.1.grad_ref), custom_call_target="tpu_custom_call" | custom-call | tf_op jit(solution)/shard_map/sum_gradients/pallas_call | solution.py:567
  87.1 0.8 copy.9
Async XLA Ops:
  0.0 30.9 %copy-start = (f32[2,2,128,128]{3,2,1,0:T(8,128)S(1)}, f32[2,2,128,128]{3,2,1,0:T(8,128)}, u32[]{:S(2)}) copy-start(f32[2,2,128,128]{3,2,1,0:T(8,128)} %probe.1) | copy-start | bytes 786436
  0.0 0.7 copy-start.1

commit v6 on v5

--- a/solution.py
+++ b/solution.py
@@ -470,66 +470,82 @@
     )(*[pltpu.with_memory_space_constraint(x, pltpu.HBM) for x in (obj, measured, phase, order)], offsets)
 
 
-def sum_kernel(grad_ref, out_ref, theirs, joined, parts, low_in, low_out, twin_send, twin_recv, x_send, x_recv, low_send, low_recv):
+def sum_kernel(grad_ref, out_ref, theirs, joined, from_above, raised, parts, low_in, low_out, twin_sem, z_send, z_recv, x_send, x_recv, low_sem):
     strip, pos = lax.axis_index("obj"), lax.axis_index("pos")
     x, core = pos // 2, pos % 2
     twin = (strip, x * 2 + 1 - core)
     below, above = (lax.rem(strip + 1, 16), pos), (lax.rem(strip + 15, 16), pos)
-    shared = 3 - 3 * core
-    mine = 2 * shared + 2 * core
     barrier = pltpu.get_barrier_semaphore()
     for step in range(1, 8):
         pl.semaphore_signal(barrier, inc=1, device_id=(strip, lax.rem(pos + step, 8)), device_id_type=MESH)
     for device in (below, above):
         pl.semaphore_signal(barrier, inc=1, device_id=device, device_id_type=MESH)
     pl.semaphore_wait(barrier, 9)
+
+    shared = 3 - 3 * core
+    plain = lax.rem(shared + 2, 4)
+    early = [lax.rem(shared + 1, 4), lax.rem(shared + 3, 4)]
+    lower, upper = pl.ds(SIDE, SIDE), pl.ds(0, SIDE)
+    halves = (lower, upper)
+
+    def place(pair, block):
+        return 2 * pair + 2 * core + block
+
     to_twin = pltpu.make_async_remote_copy(
-        src_ref=grad_ref.at[pl.ds(8 - 8 * core, 2)], dst_ref=theirs, send_sem=twin_send, recv_sem=twin_recv,
+        src_ref=grad_ref.at[pl.ds(8 - 8 * core, 2)], dst_ref=theirs, send_sem=twin_sem.at[0], recv_sem=twin_sem.at[1],
         device_id=twin, device_id_type=MESH,
     )
     to_twin.start()
-    halves = (pl.ds(SIDE, SIDE), pl.ds(0, SIDE))
-
-    def remote(pair, source, half, target, start):
+
+    def downward(which, block):
         return pltpu.make_async_remote_copy(
-            src_ref=source.at[:, :, halves[half]], dst_ref=parts.at[start, half], send_sem=x_send.at[pair, half],
-            recv_sem=x_recv.at[start, half], device_id=(strip, target), device_id_type=MESH,
+            src_ref=grad_ref.at[place(early[which], block), :, lower], dst_ref=from_above.at[which, block],
+            send_sem=z_send.at[which, block], recv_sem=z_recv.at[which, block], device_id=below, device_id_type=MESH,
         )
 
-    def local(source, half):
-        return pltpu.make_async_copy(source.at[:, :, halves[half]], parts.at[x, half], x_recv.at[x, half])
-
-    def give(pair, source, half):
+    for block in range(2):
+        for which in range(2):
+            downward(which, block).start()
+
+    def remote(pair, source, half, block, target, start):
+        return pltpu.make_async_remote_copy(
+            src_ref=source, dst_ref=parts.at[start, half, block], send_sem=x_send.at[pair, half, block],
+            recv_sem=x_recv.at[start, half, block], device_id=(strip, target), device_id_type=MESH,
+        )
+
+    def give(pair, source, half, block):
         target = 4 * core + pair
 
         @pl.when(target != pos)
         def _():
-            remote(pair, source, half, target, x).start()
+            remote(pair, source, half, block, target, x).start()
 
         @pl.when(target == pos)
         def _():
-            local(source, half).start()
-
-    def block_pair(pair):
-        return grad_ref.at[pl.ds(2 * pair + 2 * core, 2)]
-
-    pairs = [lax.rem(shared + step, 4) for step in range(1, 4)]
+            pltpu.make_async_copy(source, parts.at[x, half, block], x_recv.at[x, half, block]).start()
+
     for half in range(2):
-        for pair in pairs:
-            give(pair, block_pair(pair), half)
+        for block in range(2):
+            give(plain, grad_ref.at[place(plain, block), :, halves[half]], half, block)
     to_twin.wait_recv()
     for half in range(2):
+        rows = slice(SIDE, None) if half == 0 else slice(0, SIDE)
         for block in range(2):
             for plane in range(4):
-                rows = slice(SIDE, None) if half == 0 else slice(0, SIDE)
-                joined[block, plane, rows] = (
-                    grad_ref[mine + block, plane, rows].astype(jnp.float32) + theirs[block, plane, rows].astype(jnp.float32)
-                ).astype(jnp.bfloat16)
-        give(shared, joined, half)
-
-    def arrived(half):
+                own = grad_ref[place(shared, block), plane, rows].astype(jnp.float32)
+                joined[block, plane, rows] = (own + theirs[block, plane, rows].astype(jnp.float32)).astype(jnp.bfloat16)
+            give(shared, joined.at[block, :, halves[half]], half, block)
+    for block in range(2):
+        for which in range(2):
+            downward(which, block).wait_recv()
+            for plane in range(4):
+                own = grad_ref[place(early[which], block), plane, :SIDE].astype(jnp.float32)
+                raised[which, block, plane] = (own + from_above[which, block, plane].astype(jnp.float32)).astype(jnp.bfloat16)
+            give(early[which], raised.at[which, block], 1, block)
+
+    def arrived(half, block):
         for start in range(4):
-            remote(0, joined, half, pos, start).wait_recv()
+            remote(0, joined.at[block, :, upper], half, block, pos, start).wait_recv()
 
     def total(half, block, plane):
         value = parts[0, half, block, plane].astype(jnp.float32)
@@ -537,28 +553,43 @@
             value += parts[start, half, block, plane].astype(jnp.float32)
         return value
 
-    arrived(0)
+    shift = pltpu.make_async_remote_copy(
+        src_ref=low_out, dst_ref=low_in, send_sem=low_sem.at[0], recv_sem=low_sem.at[1], device_id=below, device_id_type=MESH,
+    )
+    sends_low = lax.rem(pos, 4) % 2 != pos // 4
+
+    @pl.when(sends_low)
+    def _():
+        for block in range(2):
+            arrived(0, block)
+            for plane in range(4):
+                low_out[block, plane] = total(0, block, plane).astype(jnp.bfloat16)
+        shift.start()
+
     for block in range(2):
+        arrived(1, block)
         for plane in range(4):
-            low_out[block, plane] = total(0, block, plane).astype(jnp.bfloat16)
-    shift = pltpu.make_async_remote_copy(
-        src_ref=low_out, dst_ref=low_in, send_sem=low_send, recv_sem=low_recv, device_id=below, device_id_type=MESH,
-    )
-    shift.start()
-    arrived(1)
-    shift.wait_recv()
+            out_ref[plane, :, block * SIDE : (block + 1) * SIDE] = total(1, block, plane)
+
+    @pl.when(sends_low)
+    def _():
+        shift.wait_recv()
+        for block in range(2):
+            for plane in range(4):
+                out_ref[plane, :, block * SIDE : (block + 1) * SIDE] += low_in[block, plane].astype(jnp.float32)
+        shift.wait_send()
+
+    to_twin.wait_send()
     for block in range(2):
-        for plane in range(4):
-            out_ref[plane, :, block * SIDE : (block + 1) * SIDE] = total(1, block, plane) + low_in[block, plane].astype(jnp.float32)
-    shift.wait_send()
-    to_twin.wait_send()
-    for half in range(2):
-        for pair in range(4):
-            target = 4 * core + pair
-
-            @pl.when(target != pos)
-            def _():
-                remote(pair, joined, half, target, x).wait_send()
+        for which in range(2):
+            downward(which, block).wait_send()
+    for pair, sent in ((plain, (0, 1)), (shared, (0, 1)), (early[0], (1,)), (early[1], (1,))):
+
+        @pl.when(4 * core + pair != pos)
+        def _():
+            for half in sent:
+                for block in range(2):
+                    remote(pair, joined.at[block, :, upper], half, block, twin[1], x).wait_send()
 
 
 def sum_call(grad):
@@ -572,15 +603,17 @@
         scratch_shapes=[
             pltpu.VMEM(two, jnp.bfloat16),
             pltpu.VMEM(two, jnp.bfloat16),
+            pltpu.VMEM((2, 2, 4, SIDE, SIDE), jnp.bfloat16),
+            pltpu.VMEM((2, 2, 4, SIDE, SIDE), jnp.bfloat16),
             pltpu.VMEM((4, 2, 2, 4, SIDE, SIDE), jnp.bfloat16),
             pltpu.VMEM((2, 4, SIDE, SIDE), jnp.bfloat16),
             pltpu.VMEM((2, 4, SIDE, SIDE), jnp.bfloat16),
-            dma,
-            dma,
-            dma((4, 2)),
-            dma((4, 2)),
-            dma,
-            dma,
+            dma((2,)),
+            dma((2, 2)),
+            dma((2, 2)),
+            dma((4, 2, 2)),
+            dma((4, 2, 2)),
+            dma((2,)),
         ],
         compiler_params=pltpu.CompilerParams(collective_id=1, has_side_effects=True, vmem_limit_bytes=20 * 2**20),
         name="sum_gradients",

time: 88 us -> 83.9 us (0.953)
  Pallas kernels: 86.3 us -> 81.7 us
    pallas_call x1, Pallas kernels: 29.1 us -> 25.8 us  [sum_call(): pl.pallas_call(sum_kernel, out_shape=jax.ShapeDtypeStruct((4, SIDE, 2 * S...]
    pallas_call x1, Pallas kernels: 27.2 us -> 25.8 us  [grads_call(): pl.pallas_call(grads_kernel, out_shape=jax.ShapeDtypeStruct((SPAN, 4, 2 *...]
where the time goes in v6:
time: 83.9 us; the launch traced here: 83.2 us
  Pallas kernels  81.7 us (97%)
  local copies, waits for them, and re-layouts  1.52 us (2%)
    pallas_call x1, Pallas kernels, send_call(): pl.pallas_call(send_kernel, out_shape=(jax.ShapeDtypeStruct((4, SPAN, 2 *...  30.1 us
    pallas_call x1, Pallas kernels, grads_call(): pl.pallas_call(grads_kernel, out_shape=jax.ShapeDtypeStruct((SPAN, 4, 2 *...  25.8 us
    pallas_call x1, Pallas kernels, sum_call(): pl.pallas_call(sum_kernel, out_shape=jax.ShapeDtypeStruct((4, SIDE, 2 * S...  25.8 us

profile of v6, /device:TPU:1, one launch (start us, length us, event | category | flops | bytes accessed | tf_op | source)
XLA Modules:
  0.0 83.2 jit_solution(11324883901743509909)
XLA Ops:
  0.0 0.0 copy-start
  0.0 0.0 copy-start.1
  0.0 0.7 copy-done.1
  0.7 30.1 %exchange_inputs.1 = (f32[4,10,256,128]{3,2,1,0:T(8,128)S(1)}, s16[2,16,2,128,128]{4,3,2,1,0:T(8,128)(2,1)S(1)}, s32[2,16,1,128]{3,2,1,0:T(1,128)S(1)}, f32[2,128,128]{2,1,0:T(8,128)S(1)}) custom-call(f32[4,128,2048]{2,1,0:T(8,128)} %bitcast.5, f32[16,128,128]{2,1,0:T(8,128)} %measured_ref.1, f32[128,128]{1,0:T(8,128)} %phase_hbm.1, ...), custom_call_target="tpu_custom_call" | custom-call | tf_op jit(solution)/shard_map/exchange_inputs/pallas_call | solution.py:440
  30.9 0.0 copy-done
  30.9 25.8 %window_gradients.1.grad_ref = bf16[10,4,256,128]{3,2,1,0:T(8,128)(2,1)S(1)} custom-call(f32[4,10,256,128]{3,2,1,0:T(8,128)S(1)} %get-tuple-element.9.field, s16[2,16,2,128,128]{4,3,2,1,0:T(8,128)(2,1)S(1)} %get-tuple-element.10.amp, s32[2,16,1,128]{3,2,1,0:T(1,128)S(1)} %get-tuple-element.11.meta_hbm, f32[2,2,128,128]{3,2,1,0:T(8,128)S(1)} %copy-done, ...), custom_call_target="tpu_custom_call" | custom-call | tf_op jit(solution)/shard_map/window_gradients/pallas_call | solution.py:226
  56.7 25.8 %sum_gradients.1 = f32[4,128,256]{2,1,0:T(8,128)S(1)} custom-call(bf16[10,4,256,128]{3,2,1,0:T(8,128)(2,1)S(1)} %window_gradients.1.grad_ref), custom_call_target="tpu_custom_call" | custom-call | tf_op jit(solution)/shard_map/sum_gradients/pallas_call | solution.py:598
  82.4 0.8 copy.9
Async XLA Ops:
  0.0 30.9 %copy-start = (f32[2,2,128,128]{3,2,1,0:T(8,128)S(1)}, f32[2,2,128,128]{3,2,1,0:T(8,128)}, u32[]{:S(2)}) copy-start(f32[2,2,128,128]{3,2,1,0:T(8,128)} %probe.1) | copy-start | bytes 786436
  0.0 0.7 copy-start.1

commit v7 on v6

--- a/solution.py
+++ b/solution.py
@@ -14,7 +14,7 @@
 META_TILE = (1, 128)
 PIECES = 4
 CHAINS, LAST_CHAINS = 5, 3
-K2_LIMIT = 30
+K2_LIMIT = 24
 SPAN = 10
 LOW_COL, HIGH_COL = 768, 1152
 AMP = jnp.int16
@@ -109,7 +109,7 @@
     return left[0] * right[0] + left[1] * right[1], left[0] * right[1] - left[1] * right[0]
 
 
-def grads_kernel(field, amp, meta_hbm, probe, prop_ref, waves_hbm, packed, grad, waves, meta_ref, order, sems):
+def grads_kernel(field, amp, meta_hbm, probe, prop_ref, waves_hbm, grad, waves, meta_ref, order, sems):
     core = lax.axis_index("pos") % 2
     base = 6 * core
     meta_load = pltpu.make_async_copy(meta_hbm, meta_ref, sems.at[0])
@@ -213,23 +213,16 @@
     rest = jnp.clip(count - CHAINS * full, 0, 1)
     lax.fori_loop(0, rest, functools.partial(step, LAST_CHAINS, CHAINS * full), 0)
 
-    def pack(block, _):
-        packed[block] = grad[block].astype(jnp.bfloat16)
-        return 0
-
-    lax.fori_loop(0, SPAN, pack, 0)
-
 
 def grads_call(field, amp, meta, probe, prop, waves):
     hbm = pl.BlockSpec(memory_space=pltpu.HBM)
     vmem = pl.BlockSpec(memory_space=pltpu.VMEM)
     return pl.pallas_call(
         grads_kernel,
-        out_shape=jax.ShapeDtypeStruct((SPAN, 4, 2 * SIDE, SIDE), jnp.bfloat16),
+        out_shape=jax.ShapeDtypeStruct((SPAN, 4, 2 * SIDE, SIDE), jnp.float32),
         in_specs=[vmem] * 5 + [hbm],
         out_specs=vmem,
         scratch_shapes=[
-            pltpu.VMEM((SPAN, 4, 2 * SIDE, SIDE), jnp.float32),
             pltpu.VMEM(waves.shape, jnp.bfloat16),
             pltpu.SMEM(meta.shape, jnp.int32),
             pltpu.SMEM((65,), jnp.int32),
@@ -240,8 +233,8 @@
     )(field, amp, meta, probe, prop, pltpu.with_memory_space_constraint(waves, pltpu.HBM))
 
 
-def send_kernel(obj_ref, measured_ref, phase_hbm, turn_hbm, offsets_ref, field, amp_ref, meta_ref, prop_ref,
-                wide, measured, own, phase, turn, halo_ref, codes_ref, chunk, amp_out, meta_out, local_sem, halo_send, halo_recv, shared_sem, slot_sem, twin_sem):
+def send_kernel(obj_ref, measured_ref, phase_hbm, turn_hbm, offsets_hbm, field, amp_ref, meta_ref, prop_ref,
+                offsets_ref, wide, measured, own, phase, turn, halo_ref, codes_ref, chunk, amp_out, meta_out, local_sem, halo_send, halo_recv, shared_sem, slot_sem, twin_sem):
     strip, pos = lax.axis_index("obj"), lax.axis_index("pos")
     x, core = pos // 2, pos % 2
     twin = (strip, x * 2 + 1 - core)
@@ -256,6 +249,7 @@
         pltpu.make_async_copy(phase_hbm, phase, local_sem.at[3]),
         pltpu.make_async_copy(obj_ref.at[:, :, pl.ds(pl.multiple_of(6 * core * SIDE, SIDE), SPAN * SIDE)], own, local_sem.at[4]),
     ]
+    loads.append(pltpu.make_async_copy(offsets_hbm, offsets_ref, local_sem.at[5]))
     for load in loads:
         load.start()
     barrier = pltpu.get_barrier_semaphore()
@@ -322,6 +316,7 @@
 
     lane = lax.broadcasted_iota(jnp.int32, META_TILE, 1)
     loads[1].wait()
+    loads[5].wait()
     loads[2].wait()
     turn_back = turn[...].astype(jnp.float32).T.astype(jnp.bfloat16)
 
@@ -445,9 +440,10 @@
             jax.ShapeDtypeStruct((2, 16, *META_TILE), jnp.int32),
             jax.ShapeDtypeStruct((2, SIDE, SIDE), jnp.float32),
         ),
-        in_specs=[hbm] * 4 + [pl.BlockSpec(memory_space=pltpu.SMEM)],
+        in_specs=[hbm] * 5,
         out_specs=(vmem,) * 4,
         scratch_shapes=[
+            pltpu.SMEM(offsets.shape, jnp.int32),
             pltpu.VMEM((4, SIDE, 2 * SIDE), jnp.float32),
             pltpu.VMEM(measured.shape, jnp.float32),
             pltpu.VMEM((4, SIDE, SPAN * SIDE), jnp.float32),
@@ -458,7 +454,7 @@
             pltpu.VMEM((8, SIDE, SIDE), jnp.bfloat16),
             pltpu.VMEM((16, CAP, SIDE, SIDE), AMP),
             pltpu.VMEM((16, *META_TILE), jnp.int32),
-            dma((5,)),
+            dma((6,)),
             dma((4, PIECES)),
             dma((4, PIECES)),
             dma((2,)),
@@ -467,10 +463,10 @@
         ],
         compiler_params=pltpu.CompilerParams(collective_id=0, has_side_effects=True, vmem_limit_bytes=20 * 2**20),
         name="exchange_inputs",
-    )(*[pltpu.with_memory_space_constraint(x, pltpu.HBM) for x in (obj, measured, phase, order)], offsets)
-
-
-def sum_kernel(grad_ref, out_ref, theirs, joined, from_above, raised, parts, low_in, low_out, twin_sem, z_send, z_recv, x_send, x_recv, low_sem):
+    )(*[pltpu.with_memory_space_constraint(x, pltpu.HBM) for x in (obj, measured, phase, order, offsets)])
+
+
+def sum_kernel(grad_ref, out_ref, twin_out, plain_out, down_out, theirs, joined, from_above, raised, parts, low_in, low_out, twin_sem, z_send, z_recv, x_send, x_recv, low_sem):
     strip, pos = lax.axis_index("obj"), lax.axis_index("pos")
     x, core = pos // 2, pos % 2
     twin = (strip, x * 2 + 1 - core)
@@ -480,7 +476,6 @@
         pl.semaphore_signal(barrier, inc=1, device_id=(strip, lax.rem(pos + step, 8)), device_id_type=MESH)
     for device in (below, above):
         pl.semaphore_signal(barrier, inc=1, device_id=device, device_id_type=MESH)
-    pl.semaphore_wait(barrier, 9)
 
     shared = 3 - 3 * core
     plain = lax.rem(shared + 2, 4)
@@ -491,15 +486,22 @@
     def place(pair, block):
         return 2 * pair + 2 * core + block
 
+    for block in range(2):
+        for plane in range(4):
+            twin_out[block, plane] = grad_ref[8 - 8 * core + block, plane].astype(jnp.bfloat16)
+            plain_out[block, plane] = grad_ref[place(plain, block), plane].astype(jnp.bfloat16)
+            for which in range(2):
+                down_out[which, block, plane] = grad_ref[place(early[which], block), plane, SIDE:].astype(jnp.bfloat16)
+    pl.semaphore_wait(barrier, 9)
     to_twin = pltpu.make_async_remote_copy(
-        src_ref=grad_ref.at[pl.ds(8 - 8 * core, 2)], dst_ref=theirs, send_sem=twin_sem.at[0], recv_sem=twin_sem.at[1],
+        src_ref=twin_out, dst_ref=theirs, send_sem=twin_sem.at[0], recv_sem=twin_sem.at[1],
         device_id=twin, device_id_type=MESH,
     )
     to_twin.start()
 
     def downward(which, block):
         return pltpu.make_async_remote_copy(
-            src_ref=grad_ref.at[place(early[which], block), :, lower], dst_ref=from_above.at[which, block],
+            src_ref=down_out.at[which, block], dst_ref=from_above.at[which, block],
             send_sem=z_send.at[which, block], recv_sem=z_recv.at[which, block], device_id=below, device_id_type=MESH,
         )
 
@@ -526,20 +528,20 @@
 
     for half in range(2):
         for block in range(2):
-            give(plain, grad_ref.at[place(plain, block), :, halves[half]], half, block)
+            give(plain, plain_out.at[block, :, halves[half]], half, block)
     to_twin.wait_recv()
     for half in range(2):
         rows = slice(SIDE, None) if half == 0 else slice(0, SIDE)
         for block in range(2):
             for plane in range(4):
-                own = grad_ref[place(shared, block), plane, rows].astype(jnp.float32)
+                own = grad_ref[place(shared, block), plane, rows]
                 joined[block, plane, rows] = (own + theirs[block, plane, rows].astype(jnp.float32)).astype(jnp.bfloat16)
             give(shared, joined.at[block, :, halves[half]], half, block)
     for block in range(2):
         for which in range(2):
             downward(which, block).wait_recv()
             for plane in range(4):
-                own = grad_ref[place(early[which], block), plane, :SIDE].astype(jnp.float32)
+                own = grad_ref[place(early[which], block), plane, :SIDE]
                 raised[which, block, plane] = (own + from_above[which, block, plane].astype(jnp.float32)).astype(jnp.bfloat16)
             give(early[which], raised.at[which, block], 1, block)
 
@@ -601,6 +603,9 @@
         in_specs=[pl.BlockSpec(memory_space=pltpu.VMEM)],
         out_specs=pl.BlockSpec(memory_space=pltpu.VMEM),
         scratch_shapes=[
+            pltpu.VMEM(two, jnp.bfloat16),
+            pltpu.VMEM(two, jnp.bfloat16),
+            pltpu.VMEM((2, 2, 4, SIDE, SIDE), jnp.bfloat16),
             pltpu.VMEM(two, jnp.bfloat16),
             pltpu.VMEM(two, jnp.bfloat16),
             pltpu.VMEM((2, 2, 4, SIDE, SIDE), jnp.bfloat16),

time: 83.9 us -> 84.3 us (level)
  Pallas kernels: 81.7 us -> 83.4 us
    pallas_call x1, Pallas kernels: 25.8 us -> 28.3 us  [sum_call(): pl.pallas_call(sum_kernel, out_shape=jax.ShapeDtypeStruct((4, SIDE, 2 * S...]
where the time goes in v7:
time: 84.3 us; the launch traced here: 84.2 us
  Pallas kernels  83.4 us (99%)
    pallas_call x1, Pallas kernels, send_call(): pl.pallas_call(send_kernel, out_shape=(jax.ShapeDtypeStruct((4, SPAN, 2 *...  29.6 us
    pallas_call x1, Pallas kernels, sum_call(): pl.pallas_call(sum_kernel, out_shape=jax.ShapeDtypeStruct((4, SIDE, 2 * S...  28.3 us
    pallas_call x1, Pallas kernels, grads_call(): pl.pallas_call(grads_kernel, out_shape=jax.ShapeDtypeStruct((SPAN, 4, 2 *...  25.5 us

profile of v7, /device:TPU:1, one launch (start us, length us, event | category | flops | bytes accessed | tf_op | source)
XLA Modules:
  0.0 84.2 jit_solution(7173754851434498850)
XLA Ops:
  0.0 0.0 copy-start
  0.0 29.6 %exchange_inputs.1 = (f32[4,10,256,128]{3,2,1,0:T(8,128)S(1)}, s16[2,16,2,128,128]{4,3,2,1,0:T(8,128)(2,1)S(1)}, s32[2,16,1,128]{3,2,1,0:T(1,128)S(1)}, f32[2,128,128]{2,1,0:T(8,128)S(1)}) custom-call(f32[4,128,2048]{2,1,0:T(8,128)} %bitcast.4, f32[16,128,128]{2,1,0:T(8,128)} %measured_ref.1, f32[128,128]{1,0:T(8,128)} %phase_hbm.1, ...), custom_call_target="tpu_custom_call" | custom-call | tf_op jit(solution)/shard_map/exchange_inputs/pallas_call | solution.py:435
  29.6 0.0 copy-done
  29.6 25.5 %window_gradients.1.grad_ref = f32[10,4,256,128]{3,2,1,0:T(8,128)S(1)} custom-call(f32[4,10,256,128]{3,2,1,0:T(8,128)S(1)} %get-tuple-element.9.field, s16[2,16,2,128,128]{4,3,2,1,0:T(8,128)(2,1)S(1)} %get-tuple-element.10.amp, s32[2,16,1,128]{3,2,1,0:T(1,128)S(1)} %get-tuple-element.11.meta_hbm, f32[2,2,128,128]{3,2,1,0:T(8,128)S(1)} %copy-done, ...), custom_call_target="tpu_custom_call" | custom-call | tf_op jit(solution)/shard_map/window_gradients/pallas_call | solution.py:220
  55.1 28.3 %sum_gradients.1 = f32[4,128,256]{2,1,0:T(8,128)S(1)} custom-call(f32[10,4,256,128]{3,2,1,0:T(8,128)S(1)} %window_gradients.1.grad_ref), custom_call_target="tpu_custom_call" | custom-call | tf_op jit(solution)/shard_map/sum_gradients/pallas_call | solution.py:600
  83.4 0.8 copy.9
Async XLA Ops:
  0.0 29.6 %copy-start = (f32[2,2,128,128]{3,2,1,0:T(8,128)S(1)}, f32[2,2,128,128]{3,2,1,0:T(8,128)}, u32[]{:S(2)}) copy-start(f32[2,2,128,128]{3,2,1,0:T(8,128)} %probe.1) | copy-start | bytes 786436

commit v8 on v7

--- a/solution.py
+++ b/solution.py
@@ -117,53 +117,44 @@
     waves_load = pltpu.make_async_copy(waves_hbm, waves, sems.at[1])
     waves_load.start()
 
+    def clear(tiles):
+        for tile in tiles:
+            grad[tile // 4, tile % 4] = jnp.zeros((2 * SIDE, SIDE), jnp.float32)
+
+    def read(slot):
+        code = meta_ref[slot >> 5, (slot >> 1) & 15, 0, slot & 1] - 1
+        return code >= 0, code >> 11, code & 2047
+
+    clear(range(2 * SPAN))
     meta_load.wait()
-
-    def read(slot):
-        code = meta_ref[slot // 32, slot % 32 // 2, 0, slot % 2] - 1
-        return code >= 0, code // 2048, code % 2048
-
-    def tally(slot, counts):
+    whole, first_only, last_only = [jnp.int32(0)] * 3
+    for slot in range(64):
         valid, _, col = read(slot)
-        here = valid.astype(jnp.int32)
-        first = here * (col < LOW_COL).astype(jnp.int32)
-        last = here * (col > HIGH_COL).astype(jnp.int32)
-        return counts[0] + here, counts[1] + first, counts[2] + last
-
-    def tally_and_clear(index, counts):
-        for k in range(8):
-            counts = tally(8 * index + k, counts)
-        for k in range(SPAN // 2):
-            tile = SPAN // 2 * index + k
-            grad[tile // 4, tile % 4] = jnp.zeros((2 * SIDE, SIDE), jnp.float32)
-        return counts
-
-    whole, first_only, last_only = lax.fori_loop(0, 8, tally_and_clear, (0, 0, 0))
-    either = whole - first_only - last_only
-    to_first = jnp.clip((whole + 1) // 2 - first_only, 0, either)
-
-    def collect(slot, state):
-        count, seen = state
+        whole = whole + valid.astype(jnp.int32)
+        first_only = first_only + (valid & (col < LOW_COL)).astype(jnp.int32)
+        last_only = last_only + (valid & (col > HIGH_COL)).astype(jnp.int32)
+    clear(range(2 * SPAN, 4 * SPAN))
+    to_first = jnp.clip(((whole + 1) >> 1) - first_only, 0, whole - first_only - last_only)
+    count, seen = jnp.int32(0), jnp.int32(0)
+    for slot in range(64):
         valid, _, col = read(slot)
         free = (col >= LOW_COL) & (col <= HIGH_COL)
         on_first = (col < LOW_COL) | (free & (seen < to_first))
-        order[count] = slot
-        mine = valid & (on_first == (core == 0))
-        return count + mine.astype(jnp.int32), seen + (valid & free).astype(jnp.int32)
-
-    count, _ = lax.fori_loop(0, 64, collect, (0, 0), unroll=8)
+        order[count] = jnp.int32(slot)
+        count = count + (valid & (on_first == (core == 0))).astype(jnp.int32)
+        seen = seen + (valid & free).astype(jnp.int32)
     waves_load.wait()
     lane = lax.broadcasted_iota(jnp.int32, (SIDE, SIDE), 1)
 
     def place(slot):
         valid, row, col = read(slot)
         row, col = jnp.where(valid, row, 0), jnp.where(valid, col, base * SIDE)
-        block, shift = jnp.clip(col // SIDE - base, 0, SPAN - 1), col % SIDE
+        block, shift = jnp.clip((col >> 7) - base, 0, SPAN - 1), col & (SIDE - 1)
         return pl.ds(row, SIDE), block, jnp.minimum(block + 1, SPAN - 1), shift
 
     def cut(plane, where):
         rows, block, next_block, shift = where
-        back = (SIDE - shift) % SIDE
+        back = (SIDE - shift) & (SIDE - 1)
         first = pltpu.roll(field[plane, block, rows, :], back, 1)
         second = pltpu.roll(field[plane, next_block, rows, :], back, 1)
         return jnp.where(lane < SIDE - shift, first, second)
@@ -185,7 +176,7 @@
         middle = yield from from_frequency(waves, [product(f, prop) for f in fields])
         far = yield from to_frequency(waves, [product(u, t1) for u in middle])
         model = 1.0 + sum(real * real + imag * imag for real, imag in far)
-        factor = weight * (1.0 - decoded(amp[slot // 32, slot % 32 // 2, slot % 2]) * lax.rsqrt(model))
+        factor = weight * (1.0 - decoded(amp[slot >> 5, (slot >> 1) & 15, slot & 1]) * lax.rsqrt(model))
         fields = yield from from_frequency(waves, [(real * factor, imag * factor) for real, imag in far])
 
         def add_slice(k, parts):

time: 84.3 us -> 80.1 us (0.950)
  the two profiles are of different devices: /device:TPU:1 before, /device:TPU:18 now
where the time goes in v8:
time: 80.1 us; the launch traced here: 78.6 us
  Pallas kernels  77.8 us (97%)
    pallas_call x1, Pallas kernels, sum_call(): pl.pallas_call(sum_kernel, out_shape=jax.ShapeDtypeStruct((4, SIDE, 2 * S...  28.4 us
    pallas_call x1, Pallas kernels, send_call(): pl.pallas_call(send_kernel, out_shape=(jax.ShapeDtypeStruct((4, SPAN, 2 *...  26.3 us
    pallas_call x1, Pallas kernels, grads_call(): pl.pallas_call(grads_kernel, out_shape=jax.ShapeDtypeStruct((SPAN, 4, 2 *...  23 us

profile of v8, /device:TPU:18, one launch (start us, length us, event | category | flops | bytes accessed | tf_op | source)
XLA Modules:
  0.0 78.6 jit_solution(9771585831892272542)
XLA Ops:
  0.0 0.0 copy-start
  0.0 26.3 %exchange_inputs.1 = (f32[4,10,256,128]{3,2,1,0:T(8,128)S(1)}, s16[2,16,2,128,128]{4,3,2,1,0:T(8,128)(2,1)S(1)}, s32[2,16,1,128]{3,2,1,0:T(1,128)S(1)}, f32[2,128,128]{2,1,0:T(8,128)S(1)}) custom-call(f32[4,128,2048]{2,1,0:T(8,128)} %bitcast.4, f32[16,128,128]{2,1,0:T(8,128)} %measured_ref.1, f32[128,128]{1,0:T(8,128)} %phase_hbm.1, ...), custom_call_target="tpu_custom_call" | custom-call | tf_op jit(solution)/shard_map/exchange_inputs/pallas_call | solution.py:426
  26.4 0.0 copy-done
  26.4 23.0 %window_gradients.1.grad_ref = f32[10,4,256,128]{3,2,1,0:T(8,128)S(1)} custom-call(f32[4,10,256,128]{3,2,1,0:T(8,128)S(1)} %get-tuple-element.9.field, s16[2,16,2,128,128]{4,3,2,1,0:T(8,128)(2,1)S(1)} %get-tuple-element.10.amp, s32[2,16,1,128]{3,2,1,0:T(1,128)S(1)} %get-tuple-element.11.meta_hbm, f32[2,2,128,128]{3,2,1,0:T(8,128)S(1)} %copy-done, ...), custom_call_target="tpu_custom_call" | custom-call | tf_op jit(solution)/shard_map/window_gradients/pallas_call | solution.py:211
  49.4 28.4 %sum_gradients.1 = f32[4,128,256]{2,1,0:T(8,128)S(1)} custom-call(f32[10,4,256,128]{3,2,1,0:T(8,128)S(1)} %window_gradients.1.grad_ref), custom_call_target="tpu_custom_call" | custom-call | tf_op jit(solution)/shard_map/sum_gradients/pallas_call | solution.py:591
  77.8 0.8 %copy.9 = f32[2,2,128,256]{3,2,1,0:T(8,128)} copy(f32[2,2,128,256]{3,2,1,0:T(8,128)S(1)} %bitcast.3) | data formatting | bytes 1048576
Async XLA Ops:
  0.0 26.4 %copy-start = (f32[2,2,128,128]{3,2,1,0:T(8,128)S(1)}, f32[2,2,128,128]{3,2,1,0:T(8,128)}, u32[]{:S(2)}) copy-start(f32[2,2,128,128]{3,2,1,0:T(8,128)} %probe.1) | copy-start | bytes 786436
